TPU v7x, 32 devices: a whole 2x2x4 slice. The times are simulated.
32 devices in a mesh: gx: 4 (over x, core), gy: 4 (over z), gz: 2 (over y).
Axes of the slice: x: 2, y: 2, z: 4, core: 2. Of those that a mesh axis runs over, the one named last changes fastest.
Arguments:
- load_data: float32 [4, 4, 2, 128, 1536], P('gx', 'gy', 'gz'), may hold values from -6 to 6
- initial_dual: float32 [4, 4, 2, 128, 1536], P('gx', 'gy', 'gz'), may hold values from -6 to 6
- dual_operator: float32 [4, 4, 2, 1536, 1536], P('gx', 'gy', 'gz'), as said below
- coarse_modes: float32 [4, 4, 2, 64, 1536], P('gx', 'gy', 'gz'), may hold values from -0.15625 to 0.15625
- coarse_inverse: float32 [2048, 2048], P(('gx', 'gy', 'gz')), as said below
- face_start: int32 [4, 4, 2, 6], P('gx', 'gy', 'gz'), may hold values from 0 to 1535, as said below
- face_len: int32 [4, 4, 2, 6], P('gx', 'gy', 'gz'), may hold values from 128 to 256, as said below
- multiplicity: int32 [4, 4, 2, 1536], P('gx', 'gy', 'gz'), may hold values from 2 to 4
Outputs:
- dual_solution: float32 [4, 4, 2, 128, 1536], P('gx', 'gy', 'gz')
- final_residual: float32 [4, 4, 2, 128, 1536], P('gx', 'gy', 'gz')
Inputs may be any that keep to these rules, and one draw needn't show every extreme that they name: `face_len`: on each subdomain the six face segments lie within 0 to 1535 and do not intersect; the pieces on the two faces that meet between neighbouring subdomains have the same length; some face between two subdomains has exactly 256 unknowns. `face_start`: start of each face segment; see face_len. `dual_operator`: each subdomain's block is symmetric. `coarse_inverse`: the matrix is symmetric.
All inputs are finite; a program needn't handle non-finite values.
Results may differ from a plain program's by a relative error of at most 0.0003.
Values sent between devices are 32-bit elements; how exact they have to be, the bound alone decides.
A program may use at most 128 MiB of HBM per device.

v0:
```python
import jax
import jax.numpy as jnp
from jax import lax
from jax.sharding import PartitionSpec as P

PCAP = 256
OUTER = 2
CHEB = 3


highest = lax.Precision.HIGHEST
center = 1.0
half_width = 0.9


def with_halo(block, sides, width):
    for axis, dim in sides:
        count = lax.axis_size(axis)
        forward = [(i, i + 1) for i in range(count - 1)]
        backward = [(target, source) for source, target in forward]
        low = lax.ppermute(
            lax.slice_in_dim(block, block.shape[dim] - width, None, axis=dim), axis, forward
        )
        high = lax.ppermute(lax.slice_in_dim(block, 0, width, axis=dim), axis, backward)
        block = jnp.concatenate([low, block, high], axis=dim)
    return block


def face_pieces(values, starts, lengths):
    padded = jnp.pad(values, ((0, 0), (0, PCAP)))
    offsets = jnp.arange(PCAP, dtype=jnp.int32)
    gathered = []
    for face_id in range(6):
        anchor = starts[face_id]
        segment = lax.dynamic_slice(padded, (jnp.int32(0), anchor), (values.shape[0], PCAP))
        gathered.append(jnp.where(offsets < lengths[face_id], segment, 0.0))
    return jnp.stack(gathered)


def place_pieces(values, received, starts, lengths):
    padded = jnp.pad(values, ((0, 0), (0, PCAP)))
    offsets = jnp.arange(PCAP, dtype=jnp.int32)
    for face_id in range(6):
        anchor = starts[face_id]
        window = lax.dynamic_slice(padded, (jnp.int32(0), anchor), (values.shape[0], PCAP))
        window = window + jnp.where(offsets < lengths[face_id], received[face_id], 0.0)
        padded = lax.dynamic_update_slice(padded, window, (jnp.int32(0), anchor))
    return padded[:, : values.shape[1]]


def per_device(
    load_data,
    initial_dual,
    dual_operator,
    coarse_modes,
    coarse_inverse,
    face_start,
    face_len,
    multiplicity,
):
    data_local = load_data[0, 0, 0]
    multipliers = initial_dual[0, 0, 0]
    operator = dual_operator[0, 0, 0]
    modes_local = coarse_modes[0, 0, 0]
    starts = face_start[0, 0, 0]
    lengths = face_len[0, 0, 0]
    inverse_weight = 1.0 / multiplicity[0, 0, 0].astype(jnp.float32)

    def operate(vectors):
        product = jnp.dot(vectors, operator, precision=highest, preferred_element_type=jnp.float32)
        pieces = face_pieces(product, starts, lengths)
        near_x = with_halo(pieces[0:2], (("gx", 0),), 1)
        near_y = with_halo(pieces[2:4], (("gy", 0),), 1)
        near_z = with_halo(pieces[4:6], (("gz", 0),), 1)
        received = jnp.stack([near_x[0], near_x[3], near_y[0], near_y[3], near_z[0], near_z[3]])
        summed = place_pieces(product, received, starts, lengths)
        return summed * inverse_weight[None, :]

    for outer_idx in range(OUTER):
        residual = data_local - operate(multipliers)
        stretch = center / half_width
        rho_now = 1.0 / stretch
        correction = residual / center
        for inner_idx in range(CHEB):
            multipliers = multipliers + correction
            if inner_idx < CHEB - 1:
                residual = residual - operate(correction)
                rho_next = 1.0 / (2.0 * stretch - rho_now)
                correction = (
                    rho_next * rho_now * correction + 2.0 * rho_next / half_width * residual
                )
                rho_now = rho_next
        coeffs = lax.dot_general(
            multipliers, modes_local, (((1,), (1,)), ((), ())), precision=highest
        )
        amplitude = lax.dot_general(
            lax.all_gather(coeffs, ("gx", "gy", "gz"), axis=1, tiled=True),
            coarse_inverse,
            (((1,), (1,)), ((), ())),
            precision=highest,
        )
        update = jnp.dot(
            amplitude, modes_local, precision=highest, preferred_element_type=jnp.float32
        )
        multipliers = multipliers - update
    final_residual = data_local - operate(multipliers)
    return (multipliers.reshape(initial_dual.shape), final_residual.reshape(initial_dual.shape))


def solution(mesh):
    placed = (
        P("gx", "gy", "gz", None, None),
        P("gx", "gy", "gz", None, None),
        P("gx", "gy", "gz", None, None),
        P("gx", "gy", "gz", None, None),
        P(("gx", "gy", "gz"), None),
        P("gx", "gy", "gz", None),
        P("gx", "gy", "gz", None),
        P("gx", "gy", "gz", None),
    )
    return jax.shard_map(
        per_device,
        mesh=mesh,
        in_specs=placed,
        out_specs=(P("gx", "gy", "gz", None, None), P("gx", "gy", "gz", None, None)),
        check_vma=False,
    )
```

profile of v0, /device:TPU:11, one launch (start us, length us, event | category | flops | bytes accessed | tf_op | source)
XLA Modules:
  0.0 491.5 jit_solution(12554215603037652623)
XLA Ops:
  22.9 8.1 %fusion.12 = f32[128,1536]{1,0:T(8,128)S(1)} fusion(f32[1,1,1,1536,1536]{4,3,2,1,0:T(8,128)} %param.10, f32[1,1,1,128,1536]{4,3,2,1,0:T(8,128)} %param.9), kind=kOutput, calls=%fused_computation.12 | convolution fusion | flops 3623878656 | bytes 11010048 | tf_op jit(solution)/shard_map/dot_general | solution.py:70
  36.6 5.5 %collective-permute-start.1 = (f32[1,128,256]{2,1,0:T(8,128)}, f32[1,128,256]{2,1,0:T(8,128)}, u32[]{:S(2)}, u32[]{:S(2)}) collective-permute-start(f32[1,128,256]{2,1,0:T(8,128)} %get-tuple-element.14), channel_id=1, source_target_pairs={{8,0},{16,8},{24,16},{9,1},{17,9},{25,17},{10,2},{18,10},{26,18},{... | collective-permute-start | bytes 393224 | tf_op jit(solution)/shard_map/ppermute | solution.py:24
  43.4 3.2 collective-permute-start.2
  46.6 2.7 collective-permute-start.3
  49.4 5.3 %collective-permute-start.4 = (f32[1,128,256]{2,1,0:T(8,128)S(1)}, f32[1,128,256]{2,1,0:T(8,128)}, u32[]{:S(2)}, u32[]{:S(2)}) collective-permute-start(f32[1,128,256]{2,1,0:T(8,128)S(1)} %get-tuple-element.50), channel_id=1, source_target_pairs={{0,1},{2,3},{4,5},{6,7},{8,9},{10,11},{12,13},{14,15},{16,17},{18,... | collective-permute-start | bytes 393224 | tf_op jit(solution)/shard_map/ppermute | solution.py:21
  68.5 7.8 %fusion.10 = f32[128,1536]{1,0:T(8,128)S(1)} fusion(f32[1,1,1,1536,1536]{4,3,2,1,0:T(8,128)} %param.10, f32[128,1792]{1,0:T(8,128)S(1)} %dynamic_update_slice.131, f32[1,1,1,128,1536]{4,3,2,1,0:T(8,128)S(1)} %copy-done.1, f32[1536]{0:T(1024)S(1)} %divide_reduce_fusion), kind=kOutput, calls=%fused_computation.10 | convolution fusion | flops 3624271872 | bytes 11804672 | tf_op jit(solution)/shard_map/dot_general | solution.py:70
  78.6 2.0 collective-permute-done.6
  81.4 6.1 %collective-permute-start.7 = (f32[1,128,256]{2,1,0:T(8,128)}, f32[1,128,256]{2,1,0:T(8,128)}, u32[]{:S(2)}, u32[]{:S(2)}) collective-permute-start(f32[1,128,256]{2,1,0:T(8,128)} %get-tuple-element.12), channel_id=1, source_target_pairs={{8,0},{16,8},{24,16},{9,1},{17,9},{25,17},{10,2},{18,10},{26,18},{... | collective-permute-start | bytes 393224 | tf_op jit(solution)/shard_map/ppermute | solution.py:24
  88.9 2.6 collective-permute-start.8
  91.5 3.3 collective-permute-start.9
  94.8 5.5 %collective-permute-start.10 = (f32[1,128,256]{2,1,0:T(8,128)S(1)}, f32[1,128,256]{2,1,0:T(8,128)}, u32[]{:S(2)}, u32[]{:S(2)}) collective-permute-start(f32[1,128,256]{2,1,0:T(8,128)S(1)} %get-tuple-element.45), channel_id=1, source_target_pairs={{0,1},{2,3},{4,5},{6,7},{8,9},{10,11},{12,13},{14,15},{16,17},{18,... | collective-permute-start | bytes 393224 | tf_op jit(solution)/shard_map/ppermute | solution.py:21
  113.3 8.0 %fusion.8 = f32[128,1536]{1,0:T(8,128)S(1)} fusion(f32[1,1,1,1536,1536]{4,3,2,1,0:T(8,128)} %param.10, f32[128,1792]{1,0:T(8,128)S(1)} %dynamic_update_slice.137, f32[1536]{0:T(1024)S(1)} %divide_reduce_fusion, f32[128,1792]{1,0:T(8,128)S(1)} %dynamic_update_slice.131, f32[1,1,1,128,1536]{4,3,2,1,0:T(8,128)S(1)} %copy-done.1), kind=kOutput, calls=%fused_computation.8 | convolution fusion | flops 3625254912 | bytes 12591104 | tf_op jit(solution)/shard_map/dot_general | solution.py:70
  124.4 1.9 collective-permute-done.12
  127.8 6.1 %collective-permute-start.13 = (f32[1,128,256]{2,1,0:T(8,128)}, f32[1,128,256]{2,1,0:T(8,128)}, u32[]{:S(2)}, u32[]{:S(2)}) collective-permute-start(f32[1,128,256]{2,1,0:T(8,128)} %get-tuple-element.10), channel_id=1, source_target_pairs={{8,0},{16,8},{24,16},{9,1},{17,9},{25,17},{10,2},{18,10},{26,18},{... | collective-permute-start | bytes 393224 | tf_op jit(solution)/shard_map/ppermute | solution.py:24
  136.2 2.1 collective-permute-start.14
  138.3 3.8 collective-permute-start.15
  142.1 5.3 %collective-permute-start.16 = (f32[1,128,256]{2,1,0:T(8,128)}, f32[1,128,256]{2,1,0:T(8,128)}, u32[]{:S(2)}, u32[]{:S(2)}) collective-permute-start(f32[1,128,256]{2,1,0:T(8,128)} %get-tuple-element.40), channel_id=1, source_target_pairs={{0,1},{2,3},{4,5},{6,7},{8,9},{10,11},{12,13},{14,15},{16,17},{18,... | collective-permute-start | bytes 393224 | tf_op jit(solution)/shard_map/ppermute | solution.py:21
  147.4 2.0 dynamic_update_slice.138
  151.1 1.9 dynamic_update_slice.139
  154.8 1.9 dynamic_update_slice.140
  158.5 1.9 dynamic_update_slice.141
  162.2 1.9 dynamic_update_slice.142
  165.9 1.9 dynamic_update_slice.143
  172.5 53.1 %all-gather.3.cloned.1.call-done = f32[128,2048]{0,1:T(8,128)} async-done(((f32[128,64]{0,1:T(8,128)}), f32[128,2048]{0,1:T(8,128)}) %all-gather.3.cloned.1.call-update) | async-done | bytes 1048592 | tf_op jit(solution)/shard_map/all_gather | solution.py:97
  225.6 3.0 fusion.95
  228.6 1.9 convolution_subtract_fusion.1
  230.6 8.1 %fusion.6 = f32[128,1536]{1,0:T(8,128)S(1)} fusion(f32[128,1536]{1,0:T(8,128)S(1)} %convolution_subtract_fusion.1, f32[1,1,1,1536,1536]{4,3,2,1,0:T(8,128)} %param.10), kind=kOutput, calls=%fused_computation.6 | convolution fusion | flops 3623878656 | bytes 11010048 | tf_op jit(solution)/shard_map/dot_general | solution.py:70
  240.3 1.9 collective-permute-done.18
  243.0 5.8 %collective-permute-start.19 = (f32[1,128,256]{2,1,0:T(8,128)}, f32[1,128,256]{2,1,0:T(8,128)}, u32[]{:S(2)}, u32[]{:S(2)}) collective-permute-start(f32[1,128,256]{2,1,0:T(8,128)} %get-tuple-element.8), channel_id=1, source_target_pairs={{8,0},{16,8},{24,16},{9,1},{17,9},{25,17},{10,2},{18,10},{26,18},{... | collective-permute-start | bytes 393224 | tf_op jit(solution)/shard_map/ppermute | solution.py:24
  250.2 2.6 collective-permute-start.20
  252.9 3.3 collective-permute-start.21
  256.2 4.0 collective-permute-start.22
  271.4 7.8 %fusion.4 = f32[128,1536]{1,0:T(8,128)S(1)} fusion(f32[1,1,1,1536,1536]{4,3,2,1,0:T(8,128)} %param.10, f32[128,1792]{1,0:T(8,128)S(1)} %dynamic_update_slice.149, f32[1,1,1,128,1536]{4,3,2,1,0:T(8,128)S(1)} %copy-done.1, f32[1536]{0:T(1024)S(1)} %divide_reduce_fusion), kind=kOutput, calls=%fused_computation.4 | convolution fusion | flops 3624271872 | bytes 11804672 | tf_op jit(solution)/shard_map/dot_general | solution.py:70
  282.2 1.9 collective-permute-done.24
  285.7 6.1 %collective-permute-start.25 = (f32[1,128,256]{2,1,0:T(8,128)}, f32[1,128,256]{2,1,0:T(8,128)}, u32[]{:S(2)}, u32[]{:S(2)}) collective-permute-start(f32[1,128,256]{2,1,0:T(8,128)} %get-tuple-element.6), channel_id=1, source_target_pairs={{8,0},{16,8},{24,16},{9,1},{17,9},{25,17},{10,2},{18,10},{26,18},{... | collective-permute-start | bytes 393224 | tf_op jit(solution)/shard_map/ppermute | solution.py:24
  293.3 2.0 collective-permute-start.26
  295.3 3.9 collective-permute-start.27
  299.2 5.3 %collective-permute-start.28 = (f32[1,128,256]{2,1,0:T(8,128)}, f32[1,128,256]{2,1,0:T(8,128)}, u32[]{:S(2)}, u32[]{:S(2)}) collective-permute-start(f32[1,128,256]{2,1,0:T(8,128)} %get-tuple-element.30), channel_id=1, source_target_pairs={{0,1},{2,3},{4,5},{6,7},{8,9},{10,11},{12,13},{14,15},{16,17},{18,... | collective-permute-start | bytes 393224 | tf_op jit(solution)/shard_map/ppermute | solution.py:21
  308.0 1.8 dynamic_update_slice.151
  311.6 1.8 dynamic_update_slice.152
  315.1 1.8 dynamic_update_slice.153
  318.6 1.8 dynamic_update_slice.154
  322.2 1.8 dynamic_update_slice.155
  324.0 8.0 %fusion.2 = f32[128,1536]{1,0:T(8,128)S(1)} fusion(f32[1,1,1,1536,1536]{4,3,2,1,0:T(8,128)} %param.10, f32[128,1792]{1,0:T(8,128)S(1)} %dynamic_update_slice.155, f32[1536]{0:T(1024)S(1)} %divide_reduce_fusion, f32[128,1792]{1,0:T(8,128)S(1)} %dynamic_update_slice.149, f32[1,1,1,128,1536]{4,3,2,1,0:T(8,128)S(1)} %copy-done.1), kind=kOutput, calls=%fused_computation.2 | convolution fusion | flops 3625254912 | bytes 12591104 | tf_op jit(solution)/shard_map/dot_general | solution.py:70
  335.0 1.9 collective-permute-done.30
  338.5 6.1 %collective-permute-start.31 = (f32[1,128,256]{2,1,0:T(8,128)}, f32[1,128,256]{2,1,0:T(8,128)}, u32[]{:S(2)}, u32[]{:S(2)}) collective-permute-start(f32[1,128,256]{2,1,0:T(8,128)} %get-tuple-element.4), channel_id=1, source_target_pairs={{8,0},{16,8},{24,16},{9,1},{17,9},{25,17},{10,2},{18,10},{26,18},{... | collective-permute-start | bytes 393224 | tf_op jit(solution)/shard_map/ppermute | solution.py:24
  346.8 1.9 collective-permute-start.32
  348.8 4.0 collective-permute-start.33
  352.8 5.3 %collective-permute-start.34 = (f32[1,128,256]{2,1,0:T(8,128)}, f32[1,128,256]{2,1,0:T(8,128)}, u32[]{:S(2)}, u32[]{:S(2)}) collective-permute-start(f32[1,128,256]{2,1,0:T(8,128)} %get-tuple-element.25), channel_id=1, source_target_pairs={{0,1},{2,3},{4,5},{6,7},{8,9},{10,11},{12,13},{14,15},{16,17},{18,... | collective-permute-start | bytes 393224 | tf_op jit(solution)/shard_map/ppermute | solution.py:21
  358.1 2.0 dynamic_update_slice.156
  361.8 1.9 dynamic_update_slice.157
  365.5 1.9 dynamic_update_slice.158
  369.1 1.9 dynamic_update_slice.159
  372.8 1.9 dynamic_update_slice.160
  376.5 1.9 dynamic_update_slice.161
  382.7 52.9 %all-gather.5.cloned.1.call-done = f32[128,2048]{0,1:T(8,128)} async-done(((f32[128,64]{0,1:T(8,128)}), f32[128,2048]{0,1:T(8,128)}) %all-gather.5.cloned.1.call-update) | async-done | bytes 1048592 | tf_op jit(solution)/shard_map/all_gather | solution.py:97
  435.6 3.0 fusion.96
  438.6 1.9 convolution_subtract_fusion
  440.5 8.1 %fusion = f32[128,1536]{1,0:T(8,128)S(1)} fusion(f32[128,1536]{1,0:T(8,128)S(1)} %convolution_subtract_fusion, f32[1,1,1,1536,1536]{4,3,2,1,0:T(8,128)} %param.10), kind=kOutput, calls=%fused_computation | convolution fusion | flops 3623878656 | bytes 11010048 | tf_op jit(solution)/shard_map/dot_general | solution.py:70
  450.9 1.9 collective-permute-done.36
  453.7 5.8 %collective-permute-start.37 = (f32[1,128,256]{2,1,0:T(8,128)}, f32[1,128,256]{2,1,0:T(8,128)}, u32[]{:S(2)}, u32[]{:S(2)}) collective-permute-start(f32[1,128,256]{2,1,0:T(8,128)} %get-tuple-element.2), channel_id=1, source_target_pairs={{8,0},{16,8},{24,16},{9,1},{17,9},{25,17},{10,2},{18,10},{26,18},{... | collective-permute-start | bytes 393224 | tf_op jit(solution)/shard_map/ppermute | solution.py:24
  460.9 2.6 collective-permute-start.38
  463.5 3.3 collective-permute-start.39
  466.8 4.7 collective-permute-start.40
  (193 shorter events, 130.3 us)
Async XLA Ops:
  7.2 218.4 %copy-start = (f32[64,2048]{1,0:T(8,128)S(1)}, f32[64,2048]{1,0:T(8,128)}, u32[]{:S(2)}) copy-start(f32[64,2048]{1,0:T(8,128)} %param.12) | copy-start | bytes 1572868
  7.2 218.4 %all-gather.3.cloned.1.call-start = ((), (), s32[]{:S(2)}) async-start(), calls=%async_computation | async-start | bytes 1081344 | tf_op jit(solution)/shard_map/all_gather | solution.py:97
  17.3 14.6 %copy-start.15 = (pred[256]{0:T(512)(128)(4,1)}, pred[256]{0:T(512)(128)(4,1)S(1)}, u32[]{:S(2)}) copy-start(pred[256]{0:T(512)(128)(4,1)S(1)} %iota_compare_fusion.4) | copy-start | bytes 772
  22.8 31.9 %copy-start.7 = (pred[256]{0:T(512)(128)(4,1)}, pred[256]{0:T(512)(128)(4,1)S(1)}, u32[]{:S(2)}) copy-start(pred[256]{0:T(512)(128)(4,1)S(1)} %get-tuple-element.65) | copy-start | bytes 772
  22.8 31.9 %copy-start.11 = (pred[256]{0:T(512)(128)(4,1)}, pred[256]{0:T(512)(128)(4,1)S(1)}, u32[]{:S(2)}) copy-start(pred[256]{0:T(512)(128)(4,1)S(1)} %get-tuple-element.66) | copy-start | bytes 772
  22.8 45.7 %copy-start.1 = (f32[1,1,1,128,1536]{4,3,2,1,0:T(8,128)S(1)}, f32[1,1,1,128,1536]{4,3,2,1,0:T(8,128)}, u32[]{:S(2)}) copy-start(f32[1,1,1,128,1536]{4,3,2,1,0:T(8,128)} %param.8) | copy-start | bytes 2359300
  31.8 4.0 collective-permute-start
  36.6 20.2 %collective-permute-start.1 = (f32[1,128,256]{2,1,0:T(8,128)}, f32[1,128,256]{2,1,0:T(8,128)}, u32[]{:S(2)}, u32[]{:S(2)}) collective-permute-start(f32[1,128,256]{2,1,0:T(8,128)} %get-tuple-element.14), channel_id=1, source_target_pairs={{8,0},{16,8},{24,16},{9,1},{17,9},{25,17},{10,2},{18,10},{26,18},{... | collective-permute-start | bytes 393224 | tf_op jit(solution)/shard_map/ppermute | solution.py:24
  42.1 24.0 %collective-permute-start.5 = (f32[1,128,256]{2,1,0:T(8,128)S(1)}, f32[1,128,256]{2,1,0:T(8,128)}, u32[]{:S(2)}, u32[]{:S(2)}) collective-permute-start(f32[1,128,256]{2,1,0:T(8,128)S(1)} %get-tuple-element.46), channel_id=1, source_target_pairs={{1,0},{3,2},{5,4},{7,6},{9,8},{11,10},{13,12},{15,14},{17,16},{19,... | collective-permute-start | bytes 393224 | tf_op jit(solution)/shard_map/ppermute | solution.py:24
  43.4 15.7 %collective-permute-start.2 = (f32[1,128,256]{2,1,0:T(8,128)}, f32[1,128,256]{2,1,0:T(8,128)}, u32[]{:S(2)}, u32[]{:S(2)}) collective-permute-start(f32[1,128,256]{2,1,0:T(8,128)} %get-tuple-element.48), channel_id=1, source_target_pairs={{0,2},{2,4},{4,6},{1,3},{3,5},{5,7},{8,10},{10,12},{12,14},{9,11},... | collective-permute-start | bytes 393224 | tf_op jit(solution)/shard_map/ppermute | solution.py:21
  46.6 14.9 %collective-permute-start.3 = (f32[1,128,256]{2,1,0:T(8,128)S(1)}, f32[1,128,256]{2,1,0:T(8,128)}, u32[]{:S(2)}, u32[]{:S(2)}) collective-permute-start(f32[1,128,256]{2,1,0:T(8,128)S(1)} %get-tuple-element.49), channel_id=1, source_target_pairs={{2,0},{4,2},{6,4},{3,1},{5,3},{7,5},{10,8},{12,10},{14,12},{11,9},... | collective-permute-start | bytes 393224 | tf_op jit(solution)/shard_map/ppermute | solution.py:24
  49.4 14.5 %collective-permute-start.4 = (f32[1,128,256]{2,1,0:T(8,128)S(1)}, f32[1,128,256]{2,1,0:T(8,128)}, u32[]{:S(2)}, u32[]{:S(2)}) collective-permute-start(f32[1,128,256]{2,1,0:T(8,128)S(1)} %get-tuple-element.50), channel_id=1, source_target_pairs={{0,1},{2,3},{4,5},{6,7},{8,9},{10,11},{12,13},{14,15},{16,17},{18,... | collective-permute-start | bytes 393224 | tf_op jit(solution)/shard_map/ppermute | solution.py:21
  54.8 21.6 %copy-start.8 = (pred[256]{0:T(512)(128)(4,1)S(1)}, pred[256]{0:T(512)(128)(4,1)}, u32[]{:S(2)}) copy-start(pred[256]{0:T(512)(128)(4,1)} %copy-done.7) | copy-start | bytes 772
  54.8 21.6 %copy-start.12 = (pred[256]{0:T(512)(128)(4,1)S(1)}, pred[256]{0:T(512)(128)(4,1)}, u32[]{:S(2)}) copy-start(pred[256]{0:T(512)(128)(4,1)} %copy-done.11) | copy-start | bytes 772
  54.8 21.6 %copy-start.16 = (pred[256]{0:T(512)(128)(4,1)S(1)}, pred[256]{0:T(512)(128)(4,1)}, u32[]{:S(2)}) copy-start(pred[256]{0:T(512)(128)(4,1)} %copy-done.15) | copy-start | bytes 772
  54.8 25.8 %copy-start.20 = (pred[256]{0:T(512)(128)(4,1)S(1)}, pred[256]{0:T(512)(128)(4,1)}, u32[]{:S(2)}) copy-start(pred[256]{0:T(512)(128)(4,1)} %copy-done.19) | copy-start | bytes 772
  77.4 3.3 collective-permute-start.6
  81.4 20.2 %collective-permute-start.7 = (f32[1,128,256]{2,1,0:T(8,128)}, f32[1,128,256]{2,1,0:T(8,128)}, u32[]{:S(2)}, u32[]{:S(2)}) collective-permute-start(f32[1,128,256]{2,1,0:T(8,128)} %get-tuple-element.12), channel_id=1, source_target_pairs={{8,0},{16,8},{24,16},{9,1},{17,9},{25,17},{10,2},{18,10},{26,18},{... | collective-permute-start | bytes 393224 | tf_op jit(solution)/shard_map/ppermute | solution.py:24
  87.6 23.4 %collective-permute-start.11 = (f32[1,128,256]{2,1,0:T(8,128)S(1)}, f32[1,128,256]{2,1,0:T(8,128)}, u32[]{:S(2)}, u32[]{:S(2)}) collective-permute-start(f32[1,128,256]{2,1,0:T(8,128)S(1)} %get-tuple-element.41), channel_id=1, source_target_pairs={{1,0},{3,2},{5,4},{7,6},{9,8},{11,10},{13,12},{15,14},{17,16},{19,... | collective-permute-start | bytes 393224 | tf_op jit(solution)/shard_map/ppermute | solution.py:24
  88.9 15.0 %collective-permute-start.8 = (f32[1,128,256]{2,1,0:T(8,128)}, f32[1,128,256]{2,1,0:T(8,128)}, u32[]{:S(2)}, u32[]{:S(2)}) collective-permute-start(f32[1,128,256]{2,1,0:T(8,128)} %get-tuple-element.43), channel_id=1, source_target_pairs={{0,2},{2,4},{4,6},{1,3},{3,5},{5,7},{8,10},{10,12},{12,14},{9,11},... | collective-permute-start | bytes 393224 | tf_op jit(solution)/shard_map/ppermute | solution.py:21
  91.5 14.8 %collective-permute-start.9 = (f32[1,128,256]{2,1,0:T(8,128)}, f32[1,128,256]{2,1,0:T(8,128)}, u32[]{:S(2)}, u32[]{:S(2)}) collective-permute-start(f32[1,128,256]{2,1,0:T(8,128)} %get-tuple-element.44), channel_id=1, source_target_pairs={{2,0},{4,2},{6,4},{3,1},{5,3},{7,5},{10,8},{12,10},{14,12},{11,9},... | collective-permute-start | bytes 393224 | tf_op jit(solution)/shard_map/ppermute | solution.py:24
  94.8 13.8 %collective-permute-start.10 = (f32[1,128,256]{2,1,0:T(8,128)S(1)}, f32[1,128,256]{2,1,0:T(8,128)}, u32[]{:S(2)}, u32[]{:S(2)}) collective-permute-start(f32[1,128,256]{2,1,0:T(8,128)S(1)} %get-tuple-element.45), channel_id=1, source_target_pairs={{0,1},{2,3},{4,5},{6,7},{8,9},{10,11},{12,13},{14,15},{16,17},{18,... | collective-permute-start | bytes 393224 | tf_op jit(solution)/shard_map/ppermute | solution.py:21
  121.3 49.1 %copy-start.5 = (f32[1,1,1,64,1536]{4,3,2,1,0:T(8,128)S(1)}, f32[1,1,1,64,1536]{4,3,2,1,0:T(8,128)}, u32[]{:S(2)}) copy-start(f32[1,1,1,64,1536]{4,3,2,1,0:T(8,128)} %param.11) | copy-start | bytes 1179652
  123.1 3.2 collective-permute-start.12
  127.8 21.6 %collective-permute-start.13 = (f32[1,128,256]{2,1,0:T(8,128)}, f32[1,128,256]{2,1,0:T(8,128)}, u32[]{:S(2)}, u32[]{:S(2)}) collective-permute-start(f32[1,128,256]{2,1,0:T(8,128)} %get-tuple-element.10), channel_id=1, source_target_pairs={{8,0},{16,8},{24,16},{9,1},{17,9},{25,17},{10,2},{18,10},{26,18},{... | collective-permute-start | bytes 393224 | tf_op jit(solution)/shard_map/ppermute | solution.py:24
  134.9 29.2 %collective-permute-start.17 = (f32[1,128,256]{2,1,0:T(8,128)}, f32[1,128,256]{2,1,0:T(8,128)}, u32[]{:S(2)}, u32[]{:S(2)}) collective-permute-start(f32[1,128,256]{2,1,0:T(8,128)} %get-tuple-element.36), channel_id=1, source_target_pairs={{1,0},{3,2},{5,4},{7,6},{9,8},{11,10},{13,12},{15,14},{17,16},{19,... | collective-permute-start | bytes 393224 | tf_op jit(solution)/shard_map/ppermute | solution.py:24
  136.2 16.9 %collective-permute-start.14 = (f32[1,128,256]{2,1,0:T(8,128)}, f32[1,128,256]{2,1,0:T(8,128)}, u32[]{:S(2)}, u32[]{:S(2)}) collective-permute-start(f32[1,128,256]{2,1,0:T(8,128)} %get-tuple-element.38), channel_id=1, source_target_pairs={{0,2},{2,4},{4,6},{1,3},{3,5},{5,7},{8,10},{10,12},{12,14},{9,11},... | collective-permute-start | bytes 393224 | tf_op jit(solution)/shard_map/ppermute | solution.py:21
  138.3 18.4 %collective-permute-start.15 = (f32[1,128,256]{2,1,0:T(8,128)}, f32[1,128,256]{2,1,0:T(8,128)}, u32[]{:S(2)}, u32[]{:S(2)}) collective-permute-start(f32[1,128,256]{2,1,0:T(8,128)} %get-tuple-element.39), channel_id=1, source_target_pairs={{2,0},{4,2},{6,4},{3,1},{5,3},{7,5},{10,8},{12,10},{14,12},{11,9},... | collective-permute-start | bytes 393224 | tf_op jit(solution)/shard_map/ppermute | solution.py:24
  142.1 18.3 %collective-permute-start.16 = (f32[1,128,256]{2,1,0:T(8,128)}, f32[1,128,256]{2,1,0:T(8,128)}, u32[]{:S(2)}, u32[]{:S(2)}) collective-permute-start(f32[1,128,256]{2,1,0:T(8,128)} %get-tuple-element.40), channel_id=1, source_target_pairs={{0,1},{2,3},{4,5},{6,7},{8,9},{10,11},{12,13},{14,15},{16,17},{18,... | collective-permute-start | bytes 393224 | tf_op jit(solution)/shard_map/ppermute | solution.py:21
  170.4 68.2 %copy-start.9 = (pred[256]{0:T(512)(128)(4,1)S(1)}, pred[256]{0:T(512)(128)(4,1)}, u32[]{:S(2)}) copy-start(pred[256]{0:T(512)(128)(4,1)} %copy-done.7) | copy-start | bytes 772
  170.4 68.2 %copy-start.13 = (pred[256]{0:T(512)(128)(4,1)S(1)}, pred[256]{0:T(512)(128)(4,1)}, u32[]{:S(2)}) copy-start(pred[256]{0:T(512)(128)(4,1)} %copy-done.11) | copy-start | bytes 772
  170.4 68.3 %copy-start.17 = (pred[256]{0:T(512)(128)(4,1)S(1)}, pred[256]{0:T(512)(128)(4,1)}, u32[]{:S(2)}) copy-start(pred[256]{0:T(512)(128)(4,1)} %copy-done.15) | copy-start | bytes 772
  170.5 71.8 %copy-start.21 = (pred[256]{0:T(512)(128)(4,1)S(1)}, pred[256]{0:T(512)(128)(4,1)}, u32[]{:S(2)}) copy-start(pred[256]{0:T(512)(128)(4,1)} %copy-done.19) | copy-start | bytes 772
  172.0 263.6 %all-gather.5.cloned.1.call-start = ((), (), s32[]{:S(2)}) async-start(), calls=%async_computation.1 | async-start | bytes 1081344 | tf_op jit(solution)/shard_map/all_gather | solution.py:97
  230.5 29.6 %copy-start.4 = (f32[128,1536]{1,0:T(8,128)}, f32[128,1536]{1,0:T(8,128)S(1)}, u32[]{:S(2)}) copy-start(f32[128,1536]{1,0:T(8,128)S(1)} %convolution_subtract_fusion.1) | copy-start | bytes 2359300
  239.0 3.2 collective-permute-start.18
  243.0 18.5 %collective-permute-start.19 = (f32[1,128,256]{2,1,0:T(8,128)}, f32[1,128,256]{2,1,0:T(8,128)}, u32[]{:S(2)}, u32[]{:S(2)}) collective-permute-start(f32[1,128,256]{2,1,0:T(8,128)} %get-tuple-element.8), channel_id=1, source_target_pairs={{8,0},{16,8},{24,16},{9,1},{17,9},{25,17},{10,2},{18,10},{26,18},{... | collective-permute-start | bytes 393224 | tf_op jit(solution)/shard_map/ppermute | solution.py:24
  248.9 21.0 %collective-permute-start.23 = (f32[1,128,256]{2,1,0:T(8,128)S(1)}, f32[1,128,256]{2,1,0:T(8,128)S(1)}, u32[]{:S(2)}, u32[]{:S(2)}) collective-permute-start(f32[1,128,256]{2,1,0:T(8,128)S(1)} %get-tuple-element.31), channel_id=1, source_target_pairs={{1,0},{3,2},{5,4},{7,6},{9,8},{11,10},{13,12},{15,14},{17,16},{19,... | collective-permute-start | bytes 393224 | tf_op jit(solution)/shard_map/ppermute | solution.py:24
  250.2 13.6 %collective-permute-start.20 = (f32[1,128,256]{2,1,0:T(8,128)S(1)}, f32[1,128,256]{2,1,0:T(8,128)}, u32[]{:S(2)}, u32[]{:S(2)}) collective-permute-start(f32[1,128,256]{2,1,0:T(8,128)S(1)} %get-tuple-element.33), channel_id=1, source_target_pairs={{0,2},{2,4},{4,6},{1,3},{3,5},{5,7},{8,10},{10,12},{12,14},{9,11},... | collective-permute-start | bytes 393224 | tf_op jit(solution)/shard_map/ppermute | solution.py:21
  252.9 13.3 %collective-permute-start.21 = (f32[1,128,256]{2,1,0:T(8,128)S(1)}, f32[1,128,256]{2,1,0:T(8,128)}, u32[]{:S(2)}, u32[]{:S(2)}) collective-permute-start(f32[1,128,256]{2,1,0:T(8,128)S(1)} %get-tuple-element.34), channel_id=1, source_target_pairs={{2,0},{4,2},{6,4},{3,1},{5,3},{7,5},{10,8},{12,10},{14,12},{11,9},... | collective-permute-start | bytes 393224 | tf_op jit(solution)/shard_map/ppermute | solution.py:24
  256.2 12.3 %collective-permute-start.22 = (f32[1,128,256]{2,1,0:T(8,128)S(1)}, f32[1,128,256]{2,1,0:T(8,128)S(1)}, u32[]{:S(2)}, u32[]{:S(2)}) collective-permute-start(f32[1,128,256]{2,1,0:T(8,128)S(1)} %get-tuple-element.35), channel_id=1, source_target_pairs={{0,1},{2,3},{4,5},{6,7},{8,9},{10,11},{12,13},{14,15},{16,17},{18,... | collective-permute-start | bytes 393224 | tf_op jit(solution)/shard_map/ppermute | solution.py:21
  281.0 3.2 collective-permute-start.24
  285.7 20.6 %collective-permute-start.25 = (f32[1,128,256]{2,1,0:T(8,128)}, f32[1,128,256]{2,1,0:T(8,128)}, u32[]{:S(2)}, u32[]{:S(2)}) collective-permute-start(f32[1,128,256]{2,1,0:T(8,128)} %get-tuple-element.6), channel_id=1, source_target_pairs={{8,0},{16,8},{24,16},{9,1},{17,9},{25,17},{10,2},{18,10},{26,18},{... | collective-permute-start | bytes 393224 | tf_op jit(solution)/shard_map/ppermute | solution.py:24
  291.8 28.6 %collective-permute-start.29 = (f32[1,128,256]{2,1,0:T(8,128)}, f32[1,128,256]{2,1,0:T(8,128)}, u32[]{:S(2)}, u32[]{:S(2)}) collective-permute-start(f32[1,128,256]{2,1,0:T(8,128)} %get-tuple-element.26), channel_id=1, source_target_pairs={{1,0},{3,2},{5,4},{7,6},{9,8},{11,10},{13,12},{15,14},{17,16},{19,... | collective-permute-start | bytes 393224 | tf_op jit(solution)/shard_map/ppermute | solution.py:24
  293.3 16.6 %collective-permute-start.26 = (f32[1,128,256]{2,1,0:T(8,128)}, f32[1,128,256]{2,1,0:T(8,128)}, u32[]{:S(2)}, u32[]{:S(2)}) collective-permute-start(f32[1,128,256]{2,1,0:T(8,128)} %get-tuple-element.28), channel_id=1, source_target_pairs={{0,2},{2,4},{4,6},{1,3},{3,5},{5,7},{8,10},{10,12},{12,14},{9,11},... | collective-permute-start | bytes 393224 | tf_op jit(solution)/shard_map/ppermute | solution.py:21
  295.3 18.1 %collective-permute-start.27 = (f32[1,128,256]{2,1,0:T(8,128)}, f32[1,128,256]{2,1,0:T(8,128)}, u32[]{:S(2)}, u32[]{:S(2)}) collective-permute-start(f32[1,128,256]{2,1,0:T(8,128)} %get-tuple-element.29), channel_id=1, source_target_pairs={{2,0},{4,2},{6,4},{3,1},{5,3},{7,5},{10,8},{12,10},{14,12},{11,9},... | collective-permute-start | bytes 393224 | tf_op jit(solution)/shard_map/ppermute | solution.py:24
  299.2 17.7 %collective-permute-start.28 = (f32[1,128,256]{2,1,0:T(8,128)}, f32[1,128,256]{2,1,0:T(8,128)}, u32[]{:S(2)}, u32[]{:S(2)}) collective-permute-start(f32[1,128,256]{2,1,0:T(8,128)} %get-tuple-element.30), channel_id=1, source_target_pairs={{0,1},{2,3},{4,5},{6,7},{8,9},{10,11},{12,13},{14,15},{16,17},{18,... | collective-permute-start | bytes 393224 | tf_op jit(solution)/shard_map/ppermute | solution.py:21
  333.7 3.2 collective-permute-start.30
  338.5 21.5 %collective-permute-start.31 = (f32[1,128,256]{2,1,0:T(8,128)}, f32[1,128,256]{2,1,0:T(8,128)}, u32[]{:S(2)}, u32[]{:S(2)}) collective-permute-start(f32[1,128,256]{2,1,0:T(8,128)} %get-tuple-element.4), channel_id=1, source_target_pairs={{8,0},{16,8},{24,16},{9,1},{17,9},{25,17},{10,2},{18,10},{26,18},{... | collective-permute-start | bytes 393224 | tf_op jit(solution)/shard_map/ppermute | solution.py:24
  345.5 29.2 %collective-permute-start.35 = (f32[1,128,256]{2,1,0:T(8,128)}, f32[1,128,256]{2,1,0:T(8,128)}, u32[]{:S(2)}, u32[]{:S(2)}) collective-permute-start(f32[1,128,256]{2,1,0:T(8,128)} %get-tuple-element.21), channel_id=1, source_target_pairs={{1,0},{3,2},{5,4},{7,6},{9,8},{11,10},{13,12},{15,14},{17,16},{19,... | collective-permute-start | bytes 393224 | tf_op jit(solution)/shard_map/ppermute | solution.py:24
  346.8 16.9 %collective-permute-start.32 = (f32[1,128,256]{2,1,0:T(8,128)}, f32[1,128,256]{2,1,0:T(8,128)}, u32[]{:S(2)}, u32[]{:S(2)}) collective-permute-start(f32[1,128,256]{2,1,0:T(8,128)} %get-tuple-element.23), channel_id=1, source_target_pairs={{0,2},{2,4},{4,6},{1,3},{3,5},{5,7},{8,10},{10,12},{12,14},{9,11},... | collective-permute-start | bytes 393224 | tf_op jit(solution)/shard_map/ppermute | solution.py:21
  348.8 18.6 %collective-permute-start.33 = (f32[1,128,256]{2,1,0:T(8,128)}, f32[1,128,256]{2,1,0:T(8,128)}, u32[]{:S(2)}, u32[]{:S(2)}) collective-permute-start(f32[1,128,256]{2,1,0:T(8,128)} %get-tuple-element.24), channel_id=1, source_target_pairs={{2,0},{4,2},{6,4},{3,1},{5,3},{7,5},{10,8},{12,10},{14,12},{11,9},... | collective-permute-start | bytes 393224 | tf_op jit(solution)/shard_map/ppermute | solution.py:24
  352.8 18.3 %collective-permute-start.34 = (f32[1,128,256]{2,1,0:T(8,128)}, f32[1,128,256]{2,1,0:T(8,128)}, u32[]{:S(2)}, u32[]{:S(2)}) collective-permute-start(f32[1,128,256]{2,1,0:T(8,128)} %get-tuple-element.25), channel_id=1, source_target_pairs={{0,1},{2,3},{4,5},{6,7},{8,9},{10,11},{12,13},{14,15},{16,17},{18,... | collective-permute-start | bytes 393224 | tf_op jit(solution)/shard_map/ppermute | solution.py:21
  381.1 67.6 %copy-start.10 = (pred[256]{0:T(512)(128)(4,1)S(1)}, pred[256]{0:T(512)(128)(4,1)}, u32[]{:S(2)}) copy-start(pred[256]{0:T(512)(128)(4,1)} %copy-done.7) | copy-start | bytes 772
  381.1 67.6 %copy-start.14 = (pred[256]{0:T(512)(128)(4,1)S(1)}, pred[256]{0:T(512)(128)(4,1)}, u32[]{:S(2)}) copy-start(pred[256]{0:T(512)(128)(4,1)} %copy-done.11) | copy-start | bytes 772
  381.1 67.6 %copy-start.18 = (pred[256]{0:T(512)(128)(4,1)S(1)}, pred[256]{0:T(512)(128)(4,1)}, u32[]{:S(2)}) copy-start(pred[256]{0:T(512)(128)(4,1)} %copy-done.15) | copy-start | bytes 772
  381.1 71.8 %copy-start.22 = (pred[256]{0:T(512)(128)(4,1)S(1)}, pred[256]{0:T(512)(128)(4,1)}, u32[]{:S(2)}) copy-start(pred[256]{0:T(512)(128)(4,1)} %copy-done.19) | copy-start | bytes 772
  440.5 43.0 %copy-start.6 = (f32[128,1536]{1,0:T(8,128)}, f32[128,1536]{1,0:T(8,128)S(1)}, u32[]{:S(2)}) copy-start(f32[128,1536]{1,0:T(8,128)S(1)} %convolution_subtract_fusion) | copy-start | bytes 2359300
  449.6 3.2 collective-permute-start.36
  453.7 19.0 %collective-permute-start.37 = (f32[1,128,256]{2,1,0:T(8,128)}, f32[1,128,256]{2,1,0:T(8,128)}, u32[]{:S(2)}, u32[]{:S(2)}) collective-permute-start(f32[1,128,256]{2,1,0:T(8,128)} %get-tuple-element.2), channel_id=1, source_target_pairs={{8,0},{16,8},{24,16},{9,1},{17,9},{25,17},{10,2},{18,10},{26,18},{... | collective-permute-start | bytes 393224 | tf_op jit(solution)/shard_map/ppermute | solution.py:24
  459.6 22.5 %collective-permute-start.41 = (f32[1,128,256]{2,1,0:T(8,128)S(1)}, f32[1,128,256]{2,1,0:T(8,128)S(1)}, u32[]{:S(2)}, u32[]{:S(2)}) collective-permute-start(f32[1,128,256]{2,1,0:T(8,128)S(1)} %get-tuple-element.16), channel_id=1, source_target_pairs={{1,0},{3,2},{5,4},{7,6},{9,8},{11,10},{13,12},{15,14},{17,16},{19,... | collective-permute-start | bytes 393224 | tf_op jit(solution)/shard_map/ppermute | solution.py:24
  460.9 14.2 %collective-permute-start.38 = (f32[1,128,256]{2,1,0:T(8,128)}, f32[1,128,256]{2,1,0:T(8,128)}, u32[]{:S(2)}, u32[]{:S(2)}) collective-permute-start(f32[1,128,256]{2,1,0:T(8,128)} %get-tuple-element.18), channel_id=1, source_target_pairs={{0,2},{2,4},{4,6},{1,3},{3,5},{5,7},{8,10},{10,12},{12,14},{9,11},... | collective-permute-start | bytes 393224 | tf_op jit(solution)/shard_map/ppermute | solution.py:21
  463.5 13.9 %collective-permute-start.39 = (f32[1,128,256]{2,1,0:T(8,128)}, f32[1,128,256]{2,1,0:T(8,128)}, u32[]{:S(2)}, u32[]{:S(2)}) collective-permute-start(f32[1,128,256]{2,1,0:T(8,128)} %get-tuple-element.19), channel_id=1, source_target_pairs={{2,0},{4,2},{6,4},{3,1},{5,3},{7,5},{10,8},{12,10},{14,12},{11,9},... | collective-permute-start | bytes 393224 | tf_op jit(solution)/shard_map/ppermute | solution.py:24
  466.8 12.9 %collective-permute-start.40 = (f32[1,128,256]{2,1,0:T(8,128)S(1)}, f32[1,128,256]{2,1,0:T(8,128)}, u32[]{:S(2)}, u32[]{:S(2)}) collective-permute-start(f32[1,128,256]{2,1,0:T(8,128)S(1)} %get-tuple-element.20), channel_id=1, source_target_pairs={{0,1},{2,3},{4,5},{6,7},{8,9},{10,11},{12,13},{14,15},{16,17},{18,... | collective-permute-start | bytes 393224 | tf_op jit(solution)/shard_map/ppermute | solution.py:21
  (3 other events, 15.3 us)
Sparse Core Ops, SparseCore 0:
  172.2 53.3 all-gather.2
  382.8 52.7 all-gather.4
where the time goes:
time: 501 us; the launch traced here: 492 us
  starting transfers between devices  137 us (27%)
  waiting for transfers between devices  118 us (24%)
  local copies, waits for them, and re-layouts  72.5 us (14%)
  matrix products  69 us (14%)
  other arithmetic  68.3 us (14%)
  between operations  27 us (5%)
    all_gather x2, waiting for transfers between devices, per_device(): lax.all_gather(coeffs, ('gx', 'gy', 'gz'), axis=1, tiled=True)  106 us
    ppermute x21, starting transfers between devices, with_halo(): lax.ppermute(lax.slice_in_dim(block, 0, width, axis=dim), axis, backward)  75.2 us
    dynamic_update_slice x42, local copies, waits for them, and re-layouts, place_pieces(): padded = lax.dynamic_update_slice(padded, window, (jnp.int32(0), anchor))  65.3 us
    ppermute x21, starting transfers between devices, with_halo(): lax.ppermute(lax.slice_in_dim(block, block.shape[dim] - width, None, axis...  61.3 us
    dot_general x7, matrix products, operate(): jnp.dot(vectors, operator, precision=highest, preferred_element_type=jnp....  56 us
    add x35, other arithmetic, place_pieces(): window + jnp.where(offsets < lengths[face_id], received[face_id], 0.0)  43.4 us
    another operation x14, other arithmetic, face_pieces(): return jnp.stack(gathered)  16 us
    ppermute x21, waiting for transfers between devices, with_halo(): lax.ppermute(lax.slice_in_dim(block, block.shape[dim] - width, None, axis...  11.7 us
  transfers between devices with their start and end apart: 44, of which 8 were waited for; matrix products, arithmetic and copies ran while one was open for 19% of the time, Pallas kernels for 0%

commit v1 on v0

v1 whole, which is shorter than its diff:
```python
import functools

import jax
import jax.numpy as jnp
from jax import lax
from jax.experimental import pallas as pl
from jax.experimental.pallas import tpu as pltpu
from jax.sharding import PartitionSpec as P

PCAP = 256
OUTER = 2
CHEB = 3
TILE = 128
SLOT = PCAP + TILE
CHUNK = 768

CENTER = 1.0
HALF_WIDTH = 0.9

F32 = jnp.float32
BF16 = jnp.bfloat16
MESH = pl.DeviceIdType.MESH
AXES = ("gx", "gy", "gz")


def split(x):
    high = x.astype(BF16)
    return high, (x - high.astype(F32)).astype(BF16)


def dot(a, b):
    return jnp.dot(a, b, preferred_element_type=F32)


def triple(a_high, a_low, cat_ref):
    width = cat_ref.shape[1] // 2
    both = dot(a_high, cat_ref[...])
    return both[:, :width] + both[:, width:] + dot(a_low, cat_ref[:, :width])


def chebyshev():
    stretch = CENTER / HALF_WIDTH
    rho = 1.0 / stretch
    out = []
    for _ in range(CHEB - 1):
        rho_next = 1.0 / (2.0 * stretch - rho)
        out.append((rho_next * rho, 2.0 * rho_next / HALF_WIDTH))
        rho = rho_next
    return out


def kernel(
    sizes,
    start_ref,
    len_ref,
    load_ref,
    first_ref,
    modes_ref,
    inverse_ref,
    mult_ref,
    operator_ref,
    dual_ref,
    final_ref,
    raw,
    op_high,
    op_low,
    product,
    load_t,
    lam,
    corr,
    res,
    weight,
    vec,
    modes_high,
    modes_low,
    modes_vec,
    modes_cat,
    image_cat,
    amp_cat,
    outgoing,
    landing,
    incoming,
    gathered,
    coeff,
    coeff_cat,
    inv_blocks,
    inv_high,
    inv_low,
    parts,
    arrived,
    places,
    raw_sem,
    halo_send,
    halo_recv,
    inv_send,
    inv_recv,
    coeff_send,
    coeff_recv,
    part_send,
    part_recv,
):
    nx, ny, nz = sizes
    m = product.shape[0] - PCAP
    loads = product.shape[1]
    nm = modes_ref.shape[0]
    tiles = m // TILE
    px, py, pz = (lax.axis_index(axis) for axis in AXES)
    spot = (px, py, pz)
    plane_me = py * nz + pz
    row_copies = m // PCAP

    plane = []
    for off in range(1, ny * nz):
        oy, oz = off // nz, off % nz
        plane.append({"gy": lax.rem(py + oy, ny), "gz": lax.rem(pz + oz, nz)})
    line = [lax.rem(px + off, nx) for off in range(1, nx)]

    barrier = pltpu.get_barrier_semaphore()
    for target in plane:
        pl.semaphore_signal(barrier, inc=1, device_id=target, device_id_type=MESH)
    for target in line:
        pl.semaphore_signal(barrier, inc=1, device_id={"gx": target}, device_id_type=MESH)

    def raw_copy(i):
        rows = pl.ds(i * PCAP, PCAP)
        return pltpu.make_async_copy(operator_ref.at[rows], raw.at[rows], raw_sem.at[i])

    for i in range(row_copies):
        raw_copy(i).start()

    lane = lax.broadcasted_iota(jnp.int32, (TILE, TILE), 1)
    for t in range(tiles):
        cols = slice(t * TILE, (t + 1) * TILE)
        load_t[cols, :] = load_ref[:, cols].T
        start_vec = first_ref[:, cols].T
        lam[cols, :] = start_vec
        high, low = split(start_vec)
        vec[cols, :loads] = high
        vec[cols, loads:] = low
        inverse_weight = 1.0 / mult_ref[:, cols].astype(F32)
        weight[cols, :] = jnp.broadcast_to(inverse_weight, (TILE, TILE)).T
        block = modes_ref[:, cols]
        high, low = split(block)
        modes_high[:, cols] = high
        modes_low[:, cols] = low
        twice = jnp.concatenate([block, block], axis=0).T
        high = twice.astype(BF16).astype(F32)
        low = twice - high
        modes_cat[cols, :TILE] = high.astype(BF16)
        modes_cat[cols, TILE:] = jnp.where(lane < nm, low, 0.0).astype(BF16)
        modes_vec[cols, :] = jnp.where(lane < nm, high, low).astype(BF16)
    corr[...] = jnp.zeros_like(corr)
    res[...] = jnp.zeros_like(res)
    incoming[...] = jnp.zeros_like(incoming)
    product[m:, :] = jnp.zeros((PCAP, loads), F32)

    for t in range(tiles):
        one = jnp.int32(0)
        two = jnp.int32(0)
        for f in range(6):
            rel = t * TILE - start_ref[f]
            hit = (rel > -TILE) & (rel < len_ref[f])
            at = TILE + SLOT * f + rel
            two = jnp.where(hit & (one > 0), at, two)
            one = jnp.where(hit & (one == 0), at, one)
        places[2 * t] = one
        places[2 * t + 1] = two

    pl.semaphore_wait(barrier, ny * nz - 1 + nx - 1)

    width = ny * nz * nm

    def inv_copy(i):
        cols = pl.ds(pl.multiple_of(line[i] * width, width), width)
        return pltpu.make_async_remote_copy(
            src_ref=inverse_ref.at[:, cols],
            dst_ref=inv_blocks.at[px],
            send_sem=inv_send.at[i],
            recv_sem=inv_recv.at[i],
            device_id={"gx": line[i]},
            device_id_type=MESH,
        )

    for i in range(nx - 1):
        inv_copy(i).start()
    inv_blocks[px] = inverse_ref[:, pl.ds(pl.multiple_of(px * width, width), width)]

    for i in range(row_copies):
        raw_copy(i).wait()

        @pl.loop(0, PCAP // 32)
        def _(k):
            rows = pl.ds(pl.multiple_of(i * PCAP + k * 32, 32), 32)
            high, low = split(raw[rows, :])
            op_high[rows, :] = high
            op_low[rows, :] = low

    def halo_copy(f, parity, arriving):
        dim, up = f // 2, f % 2
        near = spot[dim] + (1 if up else -1)
        slot = f if arriving else f ^ 1
        return pltpu.make_async_remote_copy(
            src_ref=outgoing.at[f],
            dst_ref=landing.at[parity, slot],
            send_sem=halo_send.at[f],
            recv_sem=halo_recv.at[parity, slot],
            device_id={AXES[dim]: near},
            device_id_type=MESH,
        )

    def has_near(f):
        dim, up = f // 2, f % 2
        return spot[dim] < sizes[dim] - 1 if up else spot[dim] > 0

    def coeff_copy(i, outer):
        return pltpu.make_async_remote_copy(
            src_ref=coeff,
            dst_ref=gathered.at[outer, plane_me],
            send_sem=coeff_send.at[i],
            recv_sem=coeff_recv.at[outer, i],
            device_id=plane[i],
            device_id_type=MESH,
        )

    def part_copy(i, outer):
        return pltpu.make_async_remote_copy(
            src_ref=parts.at[line[i]],
            dst_ref=arrived.at[outer, px],
            send_sem=part_send.at[i],
            recv_sem=part_recv.at[outer, i],
            device_id={"gx": line[i]},
            device_id_type=MESH,
        )

    coefs = chebyshev()
    steps = OUTER * CHEB
    row_in_piece = lax.broadcasted_iota(jnp.int32, (PCAP, loads), 0)

    @pl.loop(0, steps + 1)
    def _(n):
        stage = lax.rem(n, CHEB)
        parity = lax.rem(n, 2)

        @pl.loop(0, m // CHUNK)
        def _(k):
            rows = pl.ds(pl.multiple_of(k * CHUNK, CHUNK), CHUNK)
            product[rows, :] = triple(op_high[rows, :], op_low[rows, :], vec)

        @pl.when((stage == 0) & (n > 0))
        def _():
            outer = lax.div(n, CHEB) - 1

            @pl.when(outer == 0)
            def _():
                for i in range(nx - 1):
                    inv_copy(i).wait()
                for p in range(nx):
                    high, low = split(inv_blocks[p])
                    inv_high[p * nm : (p + 1) * nm, :] = high
                    inv_low[p * nm : (p + 1) * nm, :] = low

            for i in range(len(plane)):
                coeff_copy(i, outer).wait()
            for q in range(ny * nz):
                high, low = split(gathered[outer, q])
                coeff_cat[q * nm : (q + 1) * nm, :loads] = high
                coeff_cat[q * nm : (q + 1) * nm, loads:] = low
            part = triple(inv_high[...], inv_low[...], coeff_cat)
            for p in range(nx):
                parts[p] = part[p * nm : (p + 1) * nm, :]
            for i in range(nx - 1):
                part_copy(i, outer).start()
            arrived[outer, px] = parts[px]
            for i in range(nx - 1):
                part_copy(i, outer).wait()
            amp = arrived[outer, 0]
            for p in range(1, nx):
                amp = amp + arrived[outer, p]
            high, low = split(amp)
            amp_cat[0:nm, :] = high
            amp_cat[nm : 2 * nm, :] = low
            amp_cat[2 * nm : 3 * nm, :] = high
            amp_cat[3 * nm : 4 * nm, :] = jnp.zeros_like(high)
            product[0:m, :] = product[0:m, :] - dot(image_cat[...], amp_cat[...])

        for f in range(6):
            piece = product[pl.ds(start_ref[f], PCAP), :]
            outgoing[f] = jnp.where(row_in_piece < len_ref[f], piece, 0.0)

            @pl.when(has_near(f))
            def _():
                halo_copy(f, parity, False).start()

        @pl.when(n == 0)
        def _():
            @pl.loop(0, m // PCAP)
            def _(k):
                rows = pl.ds(pl.multiple_of(k * PCAP, PCAP), PCAP)
                one = dot(op_high[rows, :], modes_vec[...])
                two = dot(op_low[rows, :], modes_vec[...])
                left = lax.broadcasted_iota(jnp.int32, one.shape, 1) < nm
                image = one + pltpu.roll(one, nm, 1) + jnp.where(left, two, pltpu.roll(two, nm, 1))
                high = image.astype(BF16).astype(F32)
                image_cat[rows, :TILE] = high.astype(BF16)
                image_cat[rows, TILE:] = jnp.where(left, image - high, 0.0).astype(BF16)

        @pl.when((stage == 0) & (n > 0))
        def _():
            lam[...] = lam[...] - dot(modes_cat[...], amp_cat[...])

        for f in range(6):

            @pl.when(has_near(f))
            def _():
                halo_copy(f, parity, False).wait_send()
                halo_copy(f, parity, True).wait_recv()
                incoming[pl.ds(TILE + SLOT * f, PCAP), :] = landing[parity, f]

        keep = jnp.where(stage == 1, coefs[0][0], coefs[1][0]).astype(F32)
        keep = jnp.where(stage == 0, 0.0, keep)
        gain = jnp.where(stage == 1, coefs[0][1], coefs[1][1]).astype(F32)
        gain = jnp.where(stage == 0, 1.0, gain)
        add = jnp.where(n < steps, 1.0, 0.0).astype(F32)
        for t in range(tiles):
            rows = slice(t * TILE, (t + 1) * TILE)
            total = product[rows, :]
            total = total + incoming[pl.ds(places[2 * t], TILE), :]
            total = total + incoming[pl.ds(places[2 * t + 1], TILE), :]
            base = jnp.where(stage == 0, load_t[rows, :], res[rows, :])
            left_over = base - total * weight[rows, :]
            res[rows, :] = left_over
            step = keep * corr[rows, :] + gain * left_over
            corr[rows, :] = step
            grown = lam[rows, :] + add * step
            lam[rows, :] = grown
            high, low = split(jnp.where(stage == CHEB - 1, grown, step))
            vec[rows, :loads] = high
            vec[rows, loads:] = low

        @pl.when(stage == CHEB - 1)
        def _():
            outer = lax.div(n, CHEB)
            mine = triple(modes_high[...], modes_low[...], vec)
            coeff[...] = mine
            gathered[outer, plane_me] = mine
            for i in range(len(plane)):
                coeff_copy(i, outer).start()

    for t in range(tiles):
        cols = slice(t * TILE, (t + 1) * TILE)
        dual_ref[:, cols] = lam[cols, :].T
        final_ref[:, cols] = res[cols, :].T


def per_device(sizes, load, first, operator, modes, inverse, starts, lengths, mult):
    loads, m = load.shape[-2:]
    nm = modes.shape[-2]
    nx, ny, nz = sizes
    width = ny * nz * nm
    vmem = pl.BlockSpec(memory_space=pltpu.VMEM)
    smem = pl.BlockSpec(memory_space=pltpu.SMEM)
    dma = pltpu.SemaphoreType.DMA
    plane = max(ny * nz - 1, 1)
    line = max(nx - 1, 1)
    full = (m, loads)
    dual, final = pl.pallas_call(
        functools.partial(kernel, sizes),
        out_shape=[jax.ShapeDtypeStruct((loads, m), F32)] * 2,
        in_specs=[smem, smem] + [vmem] * 5 + [pl.BlockSpec(memory_space=pl.ANY)],
        out_specs=[vmem, vmem],
        scratch_shapes=[
            pltpu.VMEM((m, m), F32),
            pltpu.VMEM((m, m), BF16),
            pltpu.VMEM((m, m), BF16),
            pltpu.VMEM((m + PCAP, loads), F32),
            pltpu.VMEM(full, F32),
            pltpu.VMEM(full, F32),
            pltpu.VMEM(full, F32),
            pltpu.VMEM(full, F32),
            pltpu.VMEM(full, F32),
            pltpu.VMEM((m, 2 * loads), BF16),
            pltpu.VMEM((nm, m), BF16),
            pltpu.VMEM((nm, m), BF16),
            pltpu.VMEM((m, 2 * nm), BF16),
            pltpu.VMEM((m, 4 * nm), BF16),
            pltpu.VMEM((m, 4 * nm), BF16),
            pltpu.VMEM((4 * nm, loads), BF16),
            pltpu.VMEM((6, PCAP, loads), F32),
            pltpu.VMEM((2, 6, PCAP, loads), F32),
            pltpu.VMEM((6 * SLOT + TILE, loads), F32),
            pltpu.VMEM((OUTER, ny * nz, nm, loads), F32),
            pltpu.VMEM((nm, loads), F32),
            pltpu.VMEM((width, 2 * loads), BF16),
            pltpu.VMEM((nx, nm, width), F32),
            pltpu.VMEM((nx * nm, width), BF16),
            pltpu.VMEM((nx * nm, width), BF16),
            pltpu.VMEM((nx, nm, loads), F32),
            pltpu.VMEM((OUTER, nx, nm, loads), F32),
            pltpu.SMEM((2 * (m // TILE),), jnp.int32),
            dma((m // PCAP,)),
            dma((6,)),
            dma((2, 6)),
            dma((line,)),
            dma((line,)),
            dma((plane,)),
            dma((OUTER, plane)),
            dma((line,)),
            dma((OUTER, line)),
        ],
        compiler_params=pltpu.CompilerParams(
            collective_id=0, has_side_effects=True, vmem_limit_bytes=56 * 1024 * 1024
        ),
        cost_estimate=pl.CostEstimate(
            flops=2 * 3 * 7 * loads * m * m, bytes_accessed=4 * m * m, transcendentals=0
        ),
        name="feti_step",
    )(
        starts.reshape(-1),
        lengths.reshape(-1),
        load.reshape(loads, m),
        first.reshape(loads, m),
        modes.reshape(nm, m),
        inverse,
        mult.reshape(1, m),
        operator.reshape(m, m),
    )
    return dual.reshape(first.shape), final.reshape(first.shape)


def solution(mesh):
    block = P("gx", "gy", "gz", None, None)
    row = P("gx", "gy", "gz", None)
    sizes = tuple(mesh.shape[axis] for axis in AXES)
    return jax.shard_map(
        functools.partial(per_device, sizes),
        mesh=mesh,
        in_specs=(block, block, block, block, P(AXES, None), row, row, row),
        out_specs=(block, block),
        check_vma=False,
    )
```

time: 501 us -> 88.5 us (0.18)
  the two profiles are of different devices: /device:TPU:11 before, /device:TPU:0 now
where the time goes in v1:
time: 88.5 us; the launch traced here: 88.3 us
  Pallas kernels  83.5 us (94%)
  local copies, waits for them, and re-layouts  4.14 us (5%)
    pallas_call x1, Pallas kernels, per_device(): pl.pallas_call(functools.partial(kernel, sizes), out_shape=[jax.ShapeDtyp...  83.5 us
    unnamed x2, local copies, waits for them, and re-layouts  4.14 us

profile of v1, /device:TPU:0, one launch (start us, length us, event | category | flops | bytes accessed | tf_op | source)
XLA Modules:
  0.0 88.3 jit_solution(14976370715835897375)
XLA Ops:
  0.6 83.5 %feti_step.1 = (f32[128,1536]{1,0:T(8,128)}, f32[128,1536]{1,0:T(8,128)}) custom-call(s32[6]{0:T(128)} %bitcast.16, s32[6]{0:T(128)} %bitcast.17, f32[128,1536]{1,0:T(8,128)} %bitcast.12, f32[128,1536]{1,0:T(8,128)} %bitcast.13, f32[64,1536]{1,0:T(8,128)} %bitcast.14, f32[64,2048]{1,0:T(8,128)} %inverse_ref.1, s32[1,1536]{1,0:T(1,128)} %bitcast.15, ...), custom_call_target="tpu_custom_call" | custom-call | flops 12683575296 | bytes 9437184 | tf_op jit(solution)/shard_map/feti_step/pallas_call | solution.py:366
  84.2 2.1 %copy.12 = f32[1,1,1,128,1536]{4,3,2,1,0:T(8,128)} copy(f32[1,1,1,128,1536]{4,3,2,1,0:T(8,128)} %bitcast.10) | data formatting | bytes 1572864
  86.3 2.1 %copy.13 = f32[1,1,1,128,1536]{4,3,2,1,0:T(8,128)} copy(f32[1,1,1,128,1536]{4,3,2,1,0:T(8,128)} %bitcast.9) | data formatting | bytes 1572864

commit v2 on v1

--- a/solution.py
+++ b/solution.py
@@ -59,16 +59,14 @@
     inverse_ref,
     mult_ref,
     operator_ref,
-    dual_ref,
-    final_ref,
+    lam,
+    res,
     raw,
     op_high,
     op_low,
     product,
     load_t,
-    lam,
     corr,
-    res,
     weight,
     vec,
     modes_high,
@@ -106,20 +104,20 @@
     tiles = m // TILE
     px, py, pz = (lax.axis_index(axis) for axis in AXES)
     spot = (px, py, pz)
-    plane_me = py * nz + pz
+    plane_me = px * nz + pz
     row_copies = m // PCAP
 
     plane = []
-    for off in range(1, ny * nz):
-        oy, oz = off // nz, off % nz
-        plane.append({"gy": lax.rem(py + oy, ny), "gz": lax.rem(pz + oz, nz)})
-    line = [lax.rem(px + off, nx) for off in range(1, nx)]
+    for off in range(1, nx * nz):
+        ox, oz = off // nz, off % nz
+        plane.append({"gx": lax.rem(px + ox, nx), "gz": lax.rem(pz + oz, nz)})
+    line = [lax.rem(py + off, ny) for off in range(1, ny)]
 
     barrier = pltpu.get_barrier_semaphore()
     for target in plane:
         pl.semaphore_signal(barrier, inc=1, device_id=target, device_id_type=MESH)
     for target in line:
-        pl.semaphore_signal(barrier, inc=1, device_id={"gx": target}, device_id_type=MESH)
+        pl.semaphore_signal(barrier, inc=1, device_id={"gy": target}, device_id_type=MESH)
 
     def raw_copy(i):
         rows = pl.ds(i * PCAP, PCAP)
@@ -166,24 +164,27 @@
         places[2 * t] = one
         places[2 * t + 1] = two
 
-    pl.semaphore_wait(barrier, ny * nz - 1 + nx - 1)
-
-    width = ny * nz * nm
-
-    def inv_copy(i):
-        cols = pl.ds(pl.multiple_of(line[i] * width, width), width)
+    pl.semaphore_wait(barrier, len(plane) + len(line))
+
+    width = nz * nm
+
+    def inv_columns(p, at):
+        return pl.ds(pl.multiple_of((p * ny + at) * width, width), width)
+
+    def inv_copy(i, p):
         return pltpu.make_async_remote_copy(
-            src_ref=inverse_ref.at[:, cols],
-            dst_ref=inv_blocks.at[px],
-            send_sem=inv_send.at[i],
-            recv_sem=inv_recv.at[i],
-            device_id={"gx": line[i]},
+            src_ref=inverse_ref.at[:, inv_columns(p, line[i])],
+            dst_ref=inv_blocks.at[py, p],
+            send_sem=inv_send.at[i, p],
+            recv_sem=inv_recv.at[i, p],
+            device_id={"gy": line[i]},
             device_id_type=MESH,
         )
 
-    for i in range(nx - 1):
-        inv_copy(i).start()
-    inv_blocks[px] = inverse_ref[:, pl.ds(pl.multiple_of(px * width, width), width)]
+    for p in range(nx):
+        for i in range(len(line)):
+            inv_copy(i, p).start()
+        inv_blocks[py, p] = inverse_ref[:, inv_columns(p, py)]
 
     for i in range(row_copies):
         raw_copy(i).wait()
@@ -215,20 +216,20 @@
     def coeff_copy(i, outer):
         return pltpu.make_async_remote_copy(
             src_ref=coeff,
-            dst_ref=gathered.at[outer, plane_me],
+            dst_ref=gathered.at[outer, py],
             send_sem=coeff_send.at[i],
             recv_sem=coeff_recv.at[outer, i],
-            device_id=plane[i],
+            device_id={"gy": line[i]},
             device_id_type=MESH,
         )
 
     def part_copy(i, outer):
         return pltpu.make_async_remote_copy(
-            src_ref=parts.at[line[i]],
-            dst_ref=arrived.at[outer, px],
+            src_ref=parts.at[plane[i]["gx"] * nz + plane[i]["gz"]],
+            dst_ref=arrived.at[outer, plane_me],
             send_sem=part_send.at[i],
             recv_sem=part_recv.at[outer, i],
-            device_id={"gx": line[i]},
+            device_id=plane[i],
             device_id_type=MESH,
         )
 
@@ -252,29 +253,32 @@
 
             @pl.when(outer == 0)
             def _():
-                for i in range(nx - 1):
-                    inv_copy(i).wait()
                 for p in range(nx):
-                    high, low = split(inv_blocks[p])
-                    inv_high[p * nm : (p + 1) * nm, :] = high
-                    inv_low[p * nm : (p + 1) * nm, :] = low
-
+                    for i in range(len(line)):
+                        inv_copy(i, p).wait()
+                for p in range(nx):
+                    for z in range(0, ny, 2):
+                        pair = jnp.concatenate([inv_blocks[z, p], inv_blocks[z + 1, p]], axis=0)
+                        high, low = split(pair.T)
+                        inv_high[p * width : (p + 1) * width, z * nm : (z + 2) * nm] = high
+                        inv_low[p * width : (p + 1) * width, z * nm : (z + 2) * nm] = low
+
+            for i in range(len(line)):
+                coeff_copy(i, outer).wait()
+            for z in range(ny):
+                high, low = split(gathered[outer, z])
+                coeff_cat[z * nm : (z + 1) * nm, :loads] = high
+                coeff_cat[z * nm : (z + 1) * nm, loads:] = low
+            part = triple(inv_high[...], inv_low[...], coeff_cat)
+            for p in range(nx * nz):
+                parts[p] = part[p * nm : (p + 1) * nm, :]
             for i in range(len(plane)):
-                coeff_copy(i, outer).wait()
-            for q in range(ny * nz):
-                high, low = split(gathered[outer, q])
-                coeff_cat[q * nm : (q + 1) * nm, :loads] = high
-                coeff_cat[q * nm : (q + 1) * nm, loads:] = low
-            part = triple(inv_high[...], inv_low[...], coeff_cat)
-            for p in range(nx):
-                parts[p] = part[p * nm : (p + 1) * nm, :]
-            for i in range(nx - 1):
                 part_copy(i, outer).start()
-            arrived[outer, px] = parts[px]
-            for i in range(nx - 1):
+            arrived[outer, plane_me] = parts[plane_me]
+            for i in range(len(plane)):
                 part_copy(i, outer).wait()
             amp = arrived[outer, 0]
-            for p in range(1, nx):
+            for p in range(1, nx * nz):
                 amp = amp + arrived[outer, p]
             high, low = split(amp)
             amp_cat[0:nm, :] = high
@@ -342,30 +346,32 @@
             outer = lax.div(n, CHEB)
             mine = triple(modes_high[...], modes_low[...], vec)
             coeff[...] = mine
-            gathered[outer, plane_me] = mine
-            for i in range(len(plane)):
+            gathered[outer, py] = mine
+            for i in range(len(line)):
                 coeff_copy(i, outer).start()
 
-    for t in range(tiles):
-        cols = slice(t * TILE, (t + 1) * TILE)
-        dual_ref[:, cols] = lam[cols, :].T
-        final_ref[:, cols] = res[cols, :].T
+
+def turn(dual_t, final_t, dual_ref, final_ref):
+    for k in range(0, dual_t.shape[0], TILE):
+        cols = slice(k, k + TILE)
+        dual_ref[:, cols] = dual_t[cols, :].T
+        final_ref[:, cols] = final_t[cols, :].T
 
 
 def per_device(sizes, load, first, operator, modes, inverse, starts, lengths, mult):
     loads, m = load.shape[-2:]
     nm = modes.shape[-2]
     nx, ny, nz = sizes
-    width = ny * nz * nm
+    width = nz * nm
     vmem = pl.BlockSpec(memory_space=pltpu.VMEM)
     smem = pl.BlockSpec(memory_space=pltpu.SMEM)
     dma = pltpu.SemaphoreType.DMA
-    plane = max(ny * nz - 1, 1)
-    line = max(nx - 1, 1)
+    plane = nx * nz - 1
+    line = ny - 1
     full = (m, loads)
-    dual, final = pl.pallas_call(
+    dual_t, final_t = pl.pallas_call(
         functools.partial(kernel, sizes),
-        out_shape=[jax.ShapeDtypeStruct((loads, m), F32)] * 2,
+        out_shape=[jax.ShapeDtypeStruct(full, F32)] * 2,
         in_specs=[smem, smem] + [vmem] * 5 + [pl.BlockSpec(memory_space=pl.ANY)],
         out_specs=[vmem, vmem],
         scratch_shapes=[
@@ -373,8 +379,6 @@
             pltpu.VMEM((m, m), BF16),
             pltpu.VMEM((m, m), BF16),
             pltpu.VMEM((m + PCAP, loads), F32),
-            pltpu.VMEM(full, F32),
-            pltpu.VMEM(full, F32),
             pltpu.VMEM(full, F32),
             pltpu.VMEM(full, F32),
             pltpu.VMEM(full, F32),
@@ -388,24 +392,24 @@
             pltpu.VMEM((6, PCAP, loads), F32),
             pltpu.VMEM((2, 6, PCAP, loads), F32),
             pltpu.VMEM((6 * SLOT + TILE, loads), F32),
-            pltpu.VMEM((OUTER, ny * nz, nm, loads), F32),
+            pltpu.VMEM((OUTER, ny, nm, loads), F32),
             pltpu.VMEM((nm, loads), F32),
-            pltpu.VMEM((width, 2 * loads), BF16),
-            pltpu.VMEM((nx, nm, width), F32),
-            pltpu.VMEM((nx * nm, width), BF16),
-            pltpu.VMEM((nx * nm, width), BF16),
-            pltpu.VMEM((nx, nm, loads), F32),
-            pltpu.VMEM((OUTER, nx, nm, loads), F32),
+            pltpu.VMEM((ny * nm, 2 * loads), BF16),
+            pltpu.VMEM((ny, nx, nm, width), F32),
+            pltpu.VMEM((nx * width, ny * nm), BF16),
+            pltpu.VMEM((nx * width, ny * nm), BF16),
+            pltpu.VMEM((nx * nz, nm, loads), F32),
+            pltpu.VMEM((OUTER, nx * nz, nm, loads), F32),
             pltpu.SMEM((2 * (m // TILE),), jnp.int32),
             dma((m // PCAP,)),
             dma((6,)),
             dma((2, 6)),
+            dma((line, nx)),
+            dma((line, nx)),
             dma((line,)),
-            dma((line,)),
+            dma((OUTER, line)),
             dma((plane,)),
             dma((OUTER, plane)),
-            dma((line,)),
-            dma((OUTER, line)),
         ],
         compiler_params=pltpu.CompilerParams(
             collective_id=0, has_side_effects=True, vmem_limit_bytes=56 * 1024 * 1024
@@ -424,6 +428,17 @@
         mult.reshape(1, m),
         operator.reshape(m, m),
     )
+    step = m // 3 if m % (3 * TILE) == 0 else m
+    rows = pl.BlockSpec((step, loads), lambda k: (k, 0))
+    cols = pl.BlockSpec((loads, step), lambda k: (0, k))
+    dual, final = pl.pallas_call(
+        turn,
+        grid=(m // step,),
+        out_shape=[jax.ShapeDtypeStruct((loads, m), F32)] * 2,
+        in_specs=[rows, rows],
+        out_specs=[cols, cols],
+        name="turn",
+    )(dual_t, final_t)
     return dual.reshape(first.shape), final.reshape(first.shape)
 
 

time: 88.5 us -> 90.4 us (1.021)
  Pallas kernels: 83.5 us -> 89.5 us
  local copies, waits for them, and re-layouts: 4.14 us -> 0 us
    unnamed x2 -> x0, local copies, waits for them, and re-layouts: 4.14 us -> none
    pallas_call x0 -> x1, Pallas kernels: none -> 3.65 us  [per_device(): pl.pallas_call(turn, grid=(m // step,), out_shape=[jax.ShapeDtypeStruct((...]
    pallas_call x1, Pallas kernels: 83.5 us -> 85.8 us  [per_device(): pl.pallas_call(functools.partial(kernel, sizes), out_shape=[jax.ShapeDtyp...]
where the time goes in v2:
time: 90.4 us; the launch traced here: 90.1 us
  Pallas kernels  89.5 us (99%)
    pallas_call x1, Pallas kernels, per_device(): pl.pallas_call(functools.partial(kernel, sizes), out_shape=[jax.ShapeDtyp...  85.8 us
    pallas_call x1, Pallas kernels, per_device(): pl.pallas_call(turn, grid=(m // step,), out_shape=[jax.ShapeDtypeStruct((...  3.65 us

profile of v2, /device:TPU:0, one launch (start us, length us, event | category | flops | bytes accessed | tf_op | source)
XLA Modules:
  0.0 90.1 jit_solution(16363056048622080266)
XLA Ops:
  0.6 85.8 %feti_step.1 = (f32[1536,128]{1,0:T(8,128)}, f32[1536,128]{1,0:T(8,128)}) custom-call(s32[6]{0:T(128)} %bitcast.16, s32[6]{0:T(128)} %bitcast.17, f32[128,1536]{1,0:T(8,128)} %bitcast.10, f32[128,1536]{1,0:T(8,128)} %bitcast.11, f32[64,1536]{1,0:T(8,128)} %bitcast.14, f32[64,2048]{1,0:T(8,128)} %inverse_ref.1, s32[1,1536]{1,0:T(1,128)} %bitcast.15, ...), custom_call_target="tpu_custom_call" | custom-call | flops 12683575296 | bytes 9437184 | tf_op jit(solution)/shard_map/feti_step/pallas_call | solution.py:372
  86.5 3.6 %turn.1 = (f32[128,1536]{1,0:T(8,128)}, f32[128,1536]{1,0:T(8,128)}) custom-call(f32[1536,128]{1,0:T(8,128)} %get-tuple-element.6.dual_t, f32[1536,128]{1,0:T(8,128)} %get-tuple-element.7.final_t), custom_call_target="tpu_custom_call" | custom-call | tf_op jit(solution)/shard_map/turn/pallas_call | solution.py:434

commit v3 on v1

--- a/solution.py
+++ b/solution.py
@@ -12,7 +12,7 @@
 CHEB = 3
 TILE = 128
 SLOT = PCAP + TILE
-CHUNK = 768
+FACES = (2, 3, 4, 5, 0, 1)
 
 CENTER = 1.0
 HALF_WIDTH = 0.9
@@ -59,16 +59,14 @@
     inverse_ref,
     mult_ref,
     operator_ref,
-    dual_ref,
-    final_ref,
+    lam,
+    res,
     raw,
     op_high,
     op_low,
     product,
     load_t,
-    lam,
     corr,
-    res,
     weight,
     vec,
     modes_high,
@@ -241,10 +239,7 @@
         stage = lax.rem(n, CHEB)
         parity = lax.rem(n, 2)
 
-        @pl.loop(0, m // CHUNK)
-        def _(k):
-            rows = pl.ds(pl.multiple_of(k * CHUNK, CHUNK), CHUNK)
-            product[rows, :] = triple(op_high[rows, :], op_low[rows, :], vec)
+        product[0:m, :] = triple(op_high[...], op_low[...], vec)
 
         @pl.when((stage == 0) & (n > 0))
         def _():
@@ -283,7 +278,7 @@
             amp_cat[3 * nm : 4 * nm, :] = jnp.zeros_like(high)
             product[0:m, :] = product[0:m, :] - dot(image_cat[...], amp_cat[...])
 
-        for f in range(6):
+        for f in FACES:
             piece = product[pl.ds(start_ref[f], PCAP), :]
             outgoing[f] = jnp.where(row_in_piece < len_ref[f], piece, 0.0)
 
@@ -308,7 +303,12 @@
         def _():
             lam[...] = lam[...] - dot(modes_cat[...], amp_cat[...])
 
-        for f in range(6):
+        for t in range(tiles):
+            rows = slice(t * TILE, (t + 1) * TILE)
+            base = jnp.where(stage == 0, load_t[rows, :], res[rows, :])
+            res[rows, :] = base - product[rows, :] * weight[rows, :]
+
+        for f in reversed(FACES):
 
             @pl.when(has_near(f))
             def _():
@@ -323,11 +323,9 @@
         add = jnp.where(n < steps, 1.0, 0.0).astype(F32)
         for t in range(tiles):
             rows = slice(t * TILE, (t + 1) * TILE)
-            total = product[rows, :]
-            total = total + incoming[pl.ds(places[2 * t], TILE), :]
-            total = total + incoming[pl.ds(places[2 * t + 1], TILE), :]
-            base = jnp.where(stage == 0, load_t[rows, :], res[rows, :])
-            left_over = base - total * weight[rows, :]
+            halo = incoming[pl.ds(places[2 * t], TILE), :]
+            halo = halo + incoming[pl.ds(places[2 * t + 1], TILE), :]
+            left_over = res[rows, :] - halo * weight[rows, :]
             res[rows, :] = left_over
             step = keep * corr[rows, :] + gain * left_over
             corr[rows, :] = step
@@ -346,10 +344,12 @@
             for i in range(len(plane)):
                 coeff_copy(i, outer).start()
 
-    for t in range(tiles):
-        cols = slice(t * TILE, (t + 1) * TILE)
-        dual_ref[:, cols] = lam[cols, :].T
-        final_ref[:, cols] = res[cols, :].T
+
+def turn(dual_t, final_t, dual_ref, final_ref):
+    for k in range(0, dual_t.shape[0], TILE):
+        cols = slice(k, k + TILE)
+        dual_ref[:, cols] = dual_t[cols, :].T
+        final_ref[:, cols] = final_t[cols, :].T
 
 
 def per_device(sizes, load, first, operator, modes, inverse, starts, lengths, mult):
@@ -363,9 +363,9 @@
     plane = max(ny * nz - 1, 1)
     line = max(nx - 1, 1)
     full = (m, loads)
-    dual, final = pl.pallas_call(
+    dual_t, final_t = pl.pallas_call(
         functools.partial(kernel, sizes),
-        out_shape=[jax.ShapeDtypeStruct((loads, m), F32)] * 2,
+        out_shape=[jax.ShapeDtypeStruct(full, F32)] * 2,
         in_specs=[smem, smem] + [vmem] * 5 + [pl.BlockSpec(memory_space=pl.ANY)],
         out_specs=[vmem, vmem],
         scratch_shapes=[
@@ -373,8 +373,6 @@
             pltpu.VMEM((m, m), BF16),
             pltpu.VMEM((m, m), BF16),
             pltpu.VMEM((m + PCAP, loads), F32),
-            pltpu.VMEM(full, F32),
-            pltpu.VMEM(full, F32),
             pltpu.VMEM(full, F32),
             pltpu.VMEM(full, F32),
             pltpu.VMEM(full, F32),
@@ -424,6 +422,13 @@
         mult.reshape(1, m),
         operator.reshape(m, m),
     )
+    dual, final = pl.pallas_call(
+        turn,
+        out_shape=[jax.ShapeDtypeStruct((loads, m), F32)] * 2,
+        in_specs=[vmem, vmem],
+        out_specs=[vmem, vmem],
+        name="turn",
+    )(dual_t, final_t)
     return dual.reshape(first.shape), final.reshape(first.shape)
 
 

time: 88.5 us -> 85.3 us (0.964)
  local copies, waits for them, and re-layouts: 4.14 us -> 0 us
  Pallas kernels: 83.5 us -> 84.5 us
    unnamed x2 -> x0, local copies, waits for them, and re-layouts: 4.14 us -> none
    pallas_call x0 -> x1, Pallas kernels: none -> 2.98 us  [per_device(): pl.pallas_call(turn, out_shape=[jax.ShapeDtypeStruct((loads, m), F32)] *...]
    pallas_call x1, Pallas kernels: 83.5 us -> 81.5 us  [per_device(): pl.pallas_call(functools.partial(kernel, sizes), out_shape=[jax.ShapeDtyp...]
where the time goes in v3:
time: 85.3 us; the launch traced here: 85.1 us
  Pallas kernels  84.5 us (99%)
    pallas_call x1, Pallas kernels, per_device(): pl.pallas_call(functools.partial(kernel, sizes), out_shape=[jax.ShapeDtyp...  81.5 us
    pallas_call x1, Pallas kernels, per_device(): pl.pallas_call(turn, out_shape=[jax.ShapeDtypeStruct((loads, m), F32)] *...  2.98 us

profile of v3, /device:TPU:0, one launch (start us, length us, event | category | flops | bytes accessed | tf_op | source)
XLA Modules:
  0.0 85.1 jit_solution(4251608068365607388)
XLA Ops:
  0.6 81.5 %feti_step.1 = (f32[1536,128]{1,0:T(8,128)}, f32[1536,128]{1,0:T(8,128)}) custom-call(s32[6]{0:T(128)} %bitcast.16, s32[6]{0:T(128)} %bitcast.17, f32[128,1536]{1,0:T(8,128)} %bitcast.10, f32[128,1536]{1,0:T(8,128)} %bitcast.11, f32[64,1536]{1,0:T(8,128)} %bitcast.14, f32[64,2048]{1,0:T(8,128)} %inverse_ref.1, s32[1,1536]{1,0:T(1,128)} %bitcast.15, ...), custom_call_target="tpu_custom_call" | custom-call | flops 12683575296 | bytes 9437184 | tf_op jit(solution)/shard_map/feti_step/pallas_call | solution.py:366
  82.2 3.0 %turn.1 = (f32[128,1536]{1,0:T(8,128)}, f32[128,1536]{1,0:T(8,128)}) custom-call(f32[1536,128]{1,0:T(8,128)} %get-tuple-element.6.dual_t, f32[1536,128]{1,0:T(8,128)} %get-tuple-element.7.final_t), custom_call_target="tpu_custom_call" | custom-call | tf_op jit(solution)/shard_map/turn/pallas_call | solution.py:425

commit v4 on v3

--- a/solution.py
+++ b/solution.py
@@ -53,15 +53,21 @@
     sizes,
     start_ref,
     len_ref,
+    load_any,
+    first_any,
+    modes_any,
+    inverse_ref,
+    mult_ref,
+    operator_ref,
+    res,
+    dual_out,
+    lam,
+    raw,
     load_ref,
     first_ref,
     modes_ref,
-    inverse_ref,
-    mult_ref,
-    operator_ref,
-    lam,
-    res,
-    raw,
+    in_sem,
+    own_sem,
     op_high,
     op_low,
     product,
@@ -113,6 +119,11 @@
         plane.append({"gy": lax.rem(py + oy, ny), "gz": lax.rem(pz + oz, nz)})
     line = [lax.rem(px + off, nx) for off in range(1, nx)]
 
+    pairs = ((modes_any, modes_ref), (first_any, first_ref), (load_any, load_ref))
+    inputs = [pltpu.make_async_copy(a, b, in_sem.at[i]) for i, (a, b) in enumerate(pairs)]
+    for copy in inputs:
+        copy.start()
+
     barrier = pltpu.get_barrier_semaphore()
     for target in plane:
         pl.semaphore_signal(barrier, inc=1, device_id=target, device_id_type=MESH)
@@ -127,6 +138,8 @@
         raw_copy(i).start()
 
     lane = lax.broadcasted_iota(jnp.int32, (TILE, TILE), 1)
+    for copy in inputs:
+        copy.wait()
     for t in range(tiles):
         cols = slice(t * TILE, (t + 1) * TILE)
         load_t[cols, :] = load_ref[:, cols].T
@@ -181,7 +194,12 @@
 
     for i in range(nx - 1):
         inv_copy(i).start()
-    inv_blocks[px] = inverse_ref[:, pl.ds(pl.multiple_of(px * width, width), width)]
+    own = pltpu.make_async_copy(
+        inverse_ref.at[:, pl.ds(pl.multiple_of(px * width, width), width)],
+        inv_blocks.at[px],
+        own_sem,
+    )
+    own.start()
 
     for i in range(row_copies):
         raw_copy(i).wait()
@@ -230,6 +248,7 @@
             device_id_type=MESH,
         )
 
+    own.wait()
     coefs = chebyshev()
     steps = OUTER * CHEB
     row_in_piece = lax.broadcasted_iota(jnp.int32, (PCAP, loads), 0)
@@ -239,11 +258,12 @@
         stage = lax.rem(n, CHEB)
         parity = lax.rem(n, 2)
 
-        product[0:m, :] = triple(op_high[...], op_low[...], vec)
+        outer = lax.div(n, CHEB) - 1
+        half = m // 2
+        product[0:half, :] = triple(op_high[0:half, :], op_low[0:half, :], vec)
 
         @pl.when((stage == 0) & (n > 0))
         def _():
-            outer = lax.div(n, CHEB) - 1
 
             @pl.when(outer == 0)
             def _():
@@ -266,6 +286,11 @@
             for i in range(nx - 1):
                 part_copy(i, outer).start()
             arrived[outer, px] = parts[px]
+
+        product[half:m, :] = triple(op_high[half:m, :], op_low[half:m, :], vec)
+
+        @pl.when((stage == 0) & (n > 0))
+        def _():
             for i in range(nx - 1):
                 part_copy(i, outer).wait()
             amp = arrived[outer, 0]
@@ -302,6 +327,12 @@
         @pl.when((stage == 0) & (n > 0))
         def _():
             lam[...] = lam[...] - dot(modes_cat[...], amp_cat[...])
+
+        @pl.when(n == steps)
+        def _():
+            for t in range(tiles):
+                cols = slice(t * TILE, (t + 1) * TILE)
+                dual_out[:, cols] = lam[cols, :].T
 
         for t in range(tiles):
             rows = slice(t * TILE, (t + 1) * TILE)
@@ -345,10 +376,10 @@
                 coeff_copy(i, outer).start()
 
 
-def turn(dual_t, final_t, dual_ref, final_ref):
-    for k in range(0, dual_t.shape[0], TILE):
+def turn(dual_in, final_t, dual_ref, final_ref):
+    dual_ref[...] = dual_in[...]
+    for k in range(0, final_t.shape[0], TILE):
         cols = slice(k, k + TILE)
-        dual_ref[:, cols] = dual_t[cols, :].T
         final_ref[:, cols] = final_t[cols, :].T
 
 
@@ -358,18 +389,25 @@
     nx, ny, nz = sizes
     width = ny * nz * nm
     vmem = pl.BlockSpec(memory_space=pltpu.VMEM)
+    hbm = pl.BlockSpec(memory_space=pl.ANY)
     smem = pl.BlockSpec(memory_space=pltpu.SMEM)
     dma = pltpu.SemaphoreType.DMA
     plane = max(ny * nz - 1, 1)
     line = max(nx - 1, 1)
     full = (m, loads)
-    dual_t, final_t = pl.pallas_call(
+    final_t, dual_in = pl.pallas_call(
         functools.partial(kernel, sizes),
-        out_shape=[jax.ShapeDtypeStruct(full, F32)] * 2,
-        in_specs=[smem, smem] + [vmem] * 5 + [pl.BlockSpec(memory_space=pl.ANY)],
+        out_shape=[jax.ShapeDtypeStruct(full, F32), jax.ShapeDtypeStruct((loads, m), F32)],
+        in_specs=[smem, smem, hbm, hbm, hbm, hbm, vmem, hbm],
         out_specs=[vmem, vmem],
         scratch_shapes=[
+            pltpu.VMEM(full, F32),
             pltpu.VMEM((m, m), F32),
+            pltpu.VMEM((loads, m), F32),
+            pltpu.VMEM((loads, m), F32),
+            pltpu.VMEM((nm, m), F32),
+            dma((3,)),
+            dma,
             pltpu.VMEM((m, m), BF16),
             pltpu.VMEM((m, m), BF16),
             pltpu.VMEM((m + PCAP, loads), F32),
@@ -428,7 +466,7 @@
         in_specs=[vmem, vmem],
         out_specs=[vmem, vmem],
         name="turn",
-    )(dual_t, final_t)
+    )(dual_in, final_t)
     return dual.reshape(first.shape), final.reshape(first.shape)
 
 

time: 85.3 us -> 85.6 us (level)
  no operation moved by 1% of the time
where the time goes in v4:
time: 85.6 us; the launch traced here: 85.4 us
  Pallas kernels  84.8 us (99%)
    pallas_call x1, Pallas kernels, per_device(): pl.pallas_call(functools.partial(kernel, sizes), out_shape=[jax.ShapeDtyp...  82 us
    pallas_call x1, Pallas kernels, per_device(): pl.pallas_call(turn, out_shape=[jax.ShapeDtypeStruct((loads, m), F32)] *...  2.75 us

profile of v4, /device:TPU:0, one launch (start us, length us, event | category | flops | bytes accessed | tf_op | source)
XLA Modules:
  0.0 85.4 jit_solution(17146003686950854280)
XLA Ops:
  0.6 82.0 %feti_step.1 = (f32[1536,128]{1,0:T(8,128)}, f32[128,1536]{1,0:T(8,128)}) custom-call(s32[6]{0:T(128)} %bitcast.16, s32[6]{0:T(128)} %bitcast.17, f32[128,1536]{1,0:T(8,128)} %bitcast.10, f32[128,1536]{1,0:T(8,128)} %bitcast.11, f32[64,1536]{1,0:T(8,128)} %bitcast.14, f32[64,2048]{1,0:T(8,128)} %inverse_ref.1, s32[1,1536]{1,0:T(1,128)} %bitcast.15, ...), custom_call_target="tpu_custom_call" | custom-call | flops 12683575296 | bytes 9437184 | tf_op jit(solution)/shard_map/feti_step/pallas_call | solution.py:398
  82.7 2.7 %turn.1 = (f32[128,1536]{1,0:T(8,128)}, f32[128,1536]{1,0:T(8,128)}) custom-call(f32[128,1536]{1,0:T(8,128)} %get-tuple-element.6.dual_in, f32[1536,128]{1,0:T(8,128)} %get-tuple-element.7.final_t), custom_call_target="tpu_custom_call" | custom-call | tf_op jit(solution)/shard_map/turn/pallas_call | solution.py:463

commit v5 on v4

--- a/solution.py
+++ b/solution.py
@@ -259,8 +259,7 @@
         parity = lax.rem(n, 2)
 
         outer = lax.div(n, CHEB) - 1
-        half = m // 2
-        product[0:half, :] = triple(op_high[0:half, :], op_low[0:half, :], vec)
+        product[0:m, :] = triple(op_high[...], op_low[...], vec)
 
         @pl.when((stage == 0) & (n > 0))
         def _():
@@ -286,11 +285,6 @@
             for i in range(nx - 1):
                 part_copy(i, outer).start()
             arrived[outer, px] = parts[px]
-
-        product[half:m, :] = triple(op_high[half:m, :], op_low[half:m, :], vec)
-
-        @pl.when((stage == 0) & (n > 0))
-        def _():
             for i in range(nx - 1):
                 part_copy(i, outer).wait()
             amp = arrived[outer, 0]

time: 85.6 us -> 84.4 us (0.986)
  Pallas kernels: 84.8 us -> 83.6 us
    pallas_call x1, Pallas kernels: 82 us -> 80.9 us  [per_device(): pl.pallas_call(functools.partial(kernel, sizes), out_shape=[jax.ShapeDtyp...]
where the time goes in v5:
time: 84.4 us; the launch traced here: 84.3 us
  Pallas kernels  83.6 us (99%)
    pallas_call x1, Pallas kernels, per_device(): pl.pallas_call(functools.partial(kernel, sizes), out_shape=[jax.ShapeDtyp...  80.9 us
    pallas_call x1, Pallas kernels, per_device(): pl.pallas_call(turn, out_shape=[jax.ShapeDtypeStruct((loads, m), F32)] *...  2.75 us

profile of v5, /device:TPU:0, one launch (start us, length us, event | category | flops | bytes accessed | tf_op | source)
XLA Modules:
  0.0 84.3 jit_solution(7368877195794451894)
XLA Ops:
  0.6 80.9 %feti_step.1 = (f32[1536,128]{1,0:T(8,128)}, f32[128,1536]{1,0:T(8,128)}) custom-call(s32[6]{0:T(128)} %bitcast.16, s32[6]{0:T(128)} %bitcast.17, f32[128,1536]{1,0:T(8,128)} %bitcast.10, f32[128,1536]{1,0:T(8,128)} %bitcast.11, f32[64,1536]{1,0:T(8,128)} %bitcast.14, f32[64,2048]{1,0:T(8,128)} %inverse_ref.1, s32[1,1536]{1,0:T(1,128)} %bitcast.15, ...), custom_call_target="tpu_custom_call" | custom-call | flops 12683575296 | bytes 9437184 | tf_op jit(solution)/shard_map/feti_step/pallas_call | solution.py:392
  81.5 2.7 %turn.1 = (f32[128,1536]{1,0:T(8,128)}, f32[128,1536]{1,0:T(8,128)}) custom-call(f32[128,1536]{1,0:T(8,128)} %get-tuple-element.6.dual_in, f32[1536,128]{1,0:T(8,128)} %get-tuple-element.7.final_t), custom_call_target="tpu_custom_call" | custom-call | tf_op jit(solution)/shard_map/turn/pallas_call | solution.py:457
